TPU v7x, 32 devices: a whole 2x2x4 slice. The times are simulated.
32 devices in a mesh: seq: 4 (over x, core), batch: 8 (over z, y).
Axes of the slice: x: 2, y: 2, z: 4, core: 2. Of those that a mesh axis runs over, the one named last changes fastest.
Arguments:
- stream_in: float32 [8, 512, 512], P('batch', 'seq'), may hold values from -6 to 6
- cotangent: float32 [8, 512, 512], P('batch', 'seq'), may hold values from -6 to 6
- lengths: int32 [8], P('batch'), may hold values from 200 to 512, as said below
- norm_gain: float32 [2, 512], replicated, may hold values from 0.5 to 1.5
- decay_rate: float32 [2, 64, 512], replicated, may hold values from 0.0002 to 0.1
- in_map: float32 [2, 64, 512], replicated, may hold values from -0.6 to 0.6
- out_map: float32 [2, 64, 512], replicated, may hold values from -0.75 to 0.75
- skip_gain: float32 [2, 512], replicated, may hold values from -4 to 4
- order_two: float32 [2, 512], replicated, may hold values from -2.5 to 2.5
- step_gain: float32 [2, 512], replicated, may hold values from -4 to 4
- glu_weight: bfloat16 [2, 512, 1024], replicated, may hold values from -0.25 to 0.25
- glu_bias: float32 [2, 1024], replicated, may hold values from -1.8 to 1.8
Outputs:
- outputs: float32 [8, 512, 512], P('batch', 'seq')
- grad_input: float32 [8, 512, 512], P('batch', 'seq')
- grad_norm_gain: float32 [2, 512], replicated
- grad_decay_rate: float32 [2, 64, 512], replicated
- grad_in_map: float32 [2, 64, 512], replicated
- grad_out_map: float32 [2, 64, 512], replicated
- grad_skip_gain: float32 [2, 512], replicated
- grad_order_two: float32 [2, 512], replicated
- grad_step_gain: float32 [2, 512], replicated
- grad_glu_weight: float32 [2, 512, 1024], replicated
- grad_glu_bias: float32 [2, 1024], replicated
- stats: float32 [2, 3], replicated
Inputs may be any that keep to these rules, and one draw needn't show every extreme that they name: `lengths`: review 0 has the full length 512 and review 1 the shortest, 200.
All inputs are finite; a program needn't handle non-finite values.
Results may differ from a plain program's by a relative error of at most 0.0073.
Values sent between devices are 32-bit elements; how exact they have to be, the bound alone decides.
A program may use at most 256 MiB of HBM per device.

v0:
```python
import math

import jax
import jax.numpy as jnp
from jax import lax
from jax.sharding import PartitionSpec as P

epsilon = 1e-05
highest = lax.Precision.HIGHEST


def from_behind(x, axis, by):
    length = lax.axis_size(axis)
    pairs = [(i, i + by) for i in range(length) if 0 <= i + by < length]
    return lax.ppermute(x, axis, pairs)


def prefix(value, axis, join, neutral, backward):
    count, mine = (lax.axis_size(axis), lax.axis_index(axis))
    pieces = jax.tree.map(lambda part: lax.all_gather(part, axis), value)
    if backward:
        pieces = jax.tree.map(lambda part: part[::-1], pieces)
        mine = count - 1 - mine
    running = jax.tree.map(
        lambda part, zero: jnp.full_like(part, 0) + jnp.asarray(zero, part.dtype), value, neutral
    )

    def hop(position, running):
        longer = join(running, jax.tree.map(lambda part: part[position], pieces))
        return jax.tree.map(lambda new, old: jnp.where(position < mine, new, old), longer, running)

    return lax.fori_loop(0, count - 1, hop, running)


def layer_norm(stream, gain_row):
    center = stream - jnp.mean(stream, axis=-1, keepdims=True)
    spread = jnp.mean(center * center, axis=-1, keepdims=True)
    return center * lax.rsqrt(spread + epsilon) * gain_row


def states_scan(logs, drives, start, reverse):
    length_all = logs.shape[0]
    block_len = math.gcd(length_all, 16)
    count_blocks = length_all // block_len
    rows_idx = lax.broadcasted_iota(jnp.int32, (block_len, block_len), 0)
    cols_idx = lax.broadcasted_iota(jnp.int32, (block_len, block_len), 1)
    if reverse:
        leading = (cols_idx > rows_idx).astype(jnp.float32)
        gathering = (cols_idx >= rows_idx).astype(jnp.float32)
    else:
        leading = (cols_idx <= rows_idx).astype(jnp.float32)
        gathering = leading
    logs_blocks = logs.reshape((count_blocks, block_len) + logs.shape[1:])
    drive_blocks = drives.reshape((count_blocks, block_len) + drives.shape[1:])

    def one_block(carry, inputs):
        log_block, drive_block = inputs
        accrued = jnp.einsum("ts,snc->tnc", leading, log_block, precision=highest)
        inner = jnp.einsum(
            "ts,snc->tnc", gathering, jnp.exp(accrued) * drive_block, precision=highest
        )
        states = jnp.exp(-accrued) * (inner + carry[None])
        if reverse:
            passed = jnp.exp(-log_block[0]) * states[0]
        else:
            passed = states[-1]
        return (passed, states)

    unused, states_all = lax.scan(one_block, start, (logs_blocks, drive_blocks), reverse=reverse)
    return states_all.reshape(logs.shape)


def combine_carry(earlier, later):
    return (earlier[0] * later[0], later[1] + later[0] * earlier[1])


def local_front(stream, gain_row, step_gain, order_two, incoming):
    normed = layer_norm(stream, gain_row)
    previous = jnp.concatenate([incoming[:, None, :], normed[:, :-1, :]], axis=1)
    driven = normed + order_two * normed * previous
    rates_in = jax.nn.softplus(step_gain * normed)
    return (rates_in, driven, normed[:, -1, :])


def forward_layer(
    stream,
    valid_mask,
    gain_row,
    decay_rate,
    in_map,
    out_map,
    skip_gain,
    order_two,
    step_gain,
    weight,
    glu_bias,
):
    features = stream.shape[-1]
    normed = layer_norm(stream, gain_row)
    incoming = from_behind(normed[:, -1, :], "seq", 1)
    previous = jnp.concatenate([incoming[:, None, :], normed[:, :-1, :]], axis=1)
    driven = normed + order_two * normed * previous
    rates_in = jax.nn.softplus(step_gain * normed)
    totals = jnp.cumsum(rates_in, axis=1)
    through = jnp.exp(-decay_rate[None] * totals[:, -1, None, :])

    def local_pass(inputs):
        rates_seq, driven_seq = inputs
        logs = decay_rate[None] * rates_seq[:, None, :]
        states = states_scan(
            logs, in_map[None] * driven_seq[:, None, :], jnp.zeros_like(decay_rate), False
        )
        return (jnp.sum(out_map[None] * states, axis=1), states[-1])

    local_out, final_state = lax.map(local_pass, (rates_in, driven))
    identity = (jnp.ones_like(through), jnp.zeros_like(final_state))
    start_state = prefix((through, final_state), "seq", combine_carry, identity, False)[1]

    def correction(inputs):
        totals_seq, start_seq = inputs
        return jnp.sum(
            out_map[None] * jnp.exp(-decay_rate[None] * totals_seq[:, None, :]) * start_seq[None],
            axis=1,
        )

    mixed_out = local_out + lax.map(correction, (totals, start_state)) + skip_gain * driven
    activated = jax.nn.gelu(mixed_out)
    low_act = activated.astype(jnp.bfloat16)
    projected = (
        jnp.einsum("std,de->ste", low_act, weight, preferred_element_type=jnp.float32) + glu_bias
    )
    branch = projected[..., :features] * jax.nn.sigmoid(projected[..., features:]) * valid_mask
    result = stream + branch
    squares = jnp.stack(
        [
            jnp.sum(valid_mask * activated * activated),
            jnp.sum(branch * branch),
            jnp.sum(valid_mask * result * result),
        ]
    )
    kept = (stream, incoming, rates_in, driven, totals, start_state, mixed_out, low_act, projected)
    return (result, squares, kept)


def backward_layer(
    grad_stream,
    kept,
    valid_mask,
    gain_row,
    decay_rate,
    in_map,
    out_map,
    skip_gain,
    order_two,
    step_gain,
    weight,
):
    stream, incoming, rates_in, driven, totals, start_state, mixed_out, low_act, projected = kept
    features = stream.shape[-1]
    grad_branch = grad_stream * valid_mask
    first_half = projected[..., :features]
    gate_sig = jax.nn.sigmoid(projected[..., features:])
    grad_proj = jnp.concatenate(
        [grad_branch * gate_sig, grad_branch * first_half * gate_sig * (1.0 - gate_sig)], axis=-1
    )
    grad_bias = jnp.sum(grad_proj, axis=(0, 1))
    low_grad = grad_proj.astype(jnp.bfloat16)
    grad_weight = jnp.einsum("std,ste->de", low_act, low_grad, preferred_element_type=jnp.float32)
    grad_act = jnp.einsum("ste,de->std", low_grad, weight, preferred_element_type=jnp.float32)
    grad_mixed = jax.vjp(jax.nn.gelu, mixed_out)[1](grad_act)[0]
    grad_skip = jnp.sum(grad_mixed * driven, axis=(0, 1))
    through = jnp.exp(-decay_rate[None] * totals[:, -1, None, :])

    def adjoint_total(inputs):
        totals_seq, grad_seq = inputs
        return out_map * jnp.sum(
            jnp.exp(-decay_rate[None] * totals_seq[:, None, :]) * grad_seq[:, None, :], axis=0
        )

    pulled = lax.map(adjoint_total, (totals, grad_mixed))
    identity = (jnp.ones_like(through), jnp.zeros_like(pulled))
    arriving = prefix((through, pulled), "seq", combine_carry, identity, True)[1]

    def review_back(inputs):
        rates_seq, driven_seq, grad_seq, start_seq, arrive_seq = inputs
        logs = decay_rate[None] * rates_seq[:, None, :]
        drives = in_map[None] * driven_seq[:, None, :]
        states = states_scan(logs, drives, start_seq, False)
        sources = out_map[None] * grad_seq[:, None, :]
        adjoint = states_scan(logs, sources, arrive_seq, True)
        decay_term = adjoint * (states - drives)
        grad_rate_part = -jnp.sum(decay_term * rates_seq[:, None, :], axis=0)
        grad_rates_seq = -jnp.sum(decay_term * decay_rate[None], axis=1)
        grad_in_part = jnp.sum(adjoint * driven_seq[:, None, :], axis=0)
        grad_driven_seq = jnp.sum(in_map[None] * adjoint, axis=1)
        grad_out_part = jnp.sum(grad_seq[:, None, :] * states, axis=0)
        return (grad_rate_part, grad_in_part, grad_out_part, grad_rates_seq, grad_driven_seq)

    grad_rate, grad_in_map, grad_out_map, grad_rates_in, grad_states_in = lax.map(
        review_back, (rates_in, driven, grad_mixed, start_state, arriving)
    )
    grad_driven = skip_gain * grad_mixed + grad_states_in
    normed_first = layer_norm(stream[:, :1, :], gain_row)[:, 0, :]
    grad_previous = grad_driven[:, 0, :] * order_two * normed_first
    returned = from_behind(grad_previous, "seq", -1)
    front_back = jax.vjp(local_front, stream, gain_row, step_gain, order_two, incoming)[1]
    grad_in, grad_gain, grad_step, grad_order, unused = front_back(
        (grad_rates_in, grad_driven, returned)
    )
    layer_grads = (
        grad_gain,
        jnp.sum(grad_rate, axis=0),
        jnp.sum(grad_in_map, axis=0),
        jnp.sum(grad_out_map, axis=0),
        grad_skip,
        grad_order,
        grad_step,
        grad_weight,
        grad_bias,
    )
    return (grad_stream + grad_in, layer_grads)


def per_device(
    stream_in,
    cotangent,
    lengths,
    norm_gain,
    decay_rate,
    in_map,
    out_map,
    skip_gain,
    order_two,
    step_gain,
    glu_weight,
    glu_bias,
):
    span_len = stream_in.shape[1]
    features = stream_in.shape[2]
    layer_count = norm_gain.shape[0]
    positions = lax.axis_index("seq") * span_len + jnp.arange(span_len, dtype=jnp.int32)
    valid_mask = (positions[None, :] < lengths[:, None]).astype(jnp.float32)[:, :, None]
    stream = stream_in
    kept_all = []
    squares_all = []
    for layer_index in range(layer_count):
        stream, squares, kept = forward_layer(
            stream,
            valid_mask,
            norm_gain[layer_index],
            decay_rate[layer_index],
            in_map[layer_index],
            out_map[layer_index],
            skip_gain[layer_index],
            order_two[layer_index],
            step_gain[layer_index],
            glu_weight[layer_index],
            glu_bias[layer_index],
        )
        kept_all.append(kept)
        squares_all.append(squares)
    squares = jnp.stack(squares_all)
    valid_count = jnp.sum(valid_mask)
    squares, valid_count = lax.psum((squares, valid_count), ("seq", "batch"))
    grad_stream = cotangent
    grads_all = []
    for layer_index in range(layer_count - 1, -1, -1):
        grad_stream, layer_grads = backward_layer(
            grad_stream,
            kept_all[layer_index],
            valid_mask,
            norm_gain[layer_index],
            decay_rate[layer_index],
            in_map[layer_index],
            out_map[layer_index],
            skip_gain[layer_index],
            order_two[layer_index],
            step_gain[layer_index],
            glu_weight[layer_index],
        )
        grads_all.insert(0, layer_grads)
    stacked = [jnp.stack([layer_grads[member] for layer_grads in grads_all]) for member in range(9)]
    summed = lax.psum(
        (
            stacked[0],
            stacked[1],
            stacked[2],
            stacked[3],
            stacked[4],
            stacked[5],
            stacked[6],
            stacked[7],
            stacked[8],
        ),
        ("seq", "batch"),
    )
    stats = jnp.sqrt(squares / (valid_count * features))
    return (
        stream,
        grad_stream,
        summed[0],
        summed[1],
        summed[2],
        summed[3],
        summed[4],
        summed[5],
        summed[6],
        summed[7],
        summed[8],
        stats,
    )


def solution(mesh):
    in_specs = (
        P("batch", "seq", None),
        P("batch", "seq", None),
        P("batch"),
        P(),
        P(),
        P(),
        P(),
        P(),
        P(),
        P(),
        P(),
        P(),
    )
    out_specs = (
        P("batch", "seq", None),
        P("batch", "seq", None),
        P(),
        P(),
        P(),
        P(),
        P(),
        P(),
        P(),
        P(),
        P(),
        P(),
    )
    return jax.shard_map(
        per_device, mesh=mesh, in_specs=in_specs, out_specs=out_specs, check_vma=False
    )
```

profile of v0, /device:TPU:0, one launch (start us, length us, event | category | flops | bytes accessed | tf_op | source)
XLA Modules:
  0.0 936.4 jit_solution(14448391687077509059)
XLA Ops:
  27.8 8.0 broadcast_multiply_fusion.5
  35.7 8.0 broadcast_multiply_fusion.4
  43.8 7.9 broadcast.226.clone
  51.7 74.4 %while.208 = (s32[]{:T(128)}, f32[64,512]{1,0:T(8,128)S(1)}, f32[8,16,64,512]{3,1,2,0:T(8,128)}, f32[8,16,64,512]{3,1,2,0:T(8,128)}, f32[8,16,64,512]{3,1,2,0:T(8,128)}, /*index=5*/s32[]{:T(128)}) while((s32[]{:T(128)}, f32[64,512]{1,0:T(8,128)S(1)}, f32[8,16,64,512]{3,1,2,0:T(8,128)}, f32[8,16,64,512]{3,1,2,0:T(8,128)}, ...), condition=%wide.region_3.4_spmd.clone.clone, body=%wide.region_2.3_spmd.clone.clone.sunk | while | flops 203424768 | bytes 15337029 | solution.py:69
  126.1 15.2 %copy.46 = f32[8,16,64,512]{3,2,1,0:T(8,128)S(1)} copy(f32[8,16,64,512]{3,1,2,0:T(8,128)} %get-tuple-element.1014) | data formatting | bytes 33554432 | tf_op jit(solution)/shard_map/while/body/eval_jaxpr/while | solution.py:69
  141.3 8.2 all-gather
  158.3 8.1 multiply_reduce_fusion.15
  178.4 7.9 broadcast.226.clone.5
  186.3 74.6 %while.211 = (s32[]{:T(128)}, f32[64,512]{1,0:T(8,128)S(1)}, f32[8,16,64,512]{3,1,2,0:T(8,128)}, f32[8,16,64,512]{3,1,2,0:T(8,128)}, f32[8,16,64,512]{3,1,2,0:T(8,128)}, /*index=5*/s32[]{:T(128)}) while((s32[]{:T(128)}, f32[64,512]{1,0:T(8,128)S(1)}, f32[8,16,64,512]{3,1,2,0:T(8,128)}, ...), condition=%wide.region_40.41_spmd.clone.clone, body=%wide.region_39.40_spmd.clone.clone.sunk | while | flops 203424768 | bytes 15337029 | solution.py:69
  262.4 11.9 %broadcast_multiply_fusion.2 = (f32[8,16,64,512]{3,1,2,0:T(8,128)}, f32[8,16,64,512]{3,1,2,0:T(8,128)}) fusion(f32[8,16,512]{2,1,0:T(8,128)S(1)} %bitcast.598, f32[64,512]{1,0:T(8,128)S(1)} %get-tuple-element.1504, f32[8,16,512]{2,1,0:T(8,128)S(1)} %bitcast.606, f32[64,512]{1,0:T(8,128)S(1)} %get-tuple-element.1502), kind=kLoop, calls=%fused_computation.160 | loop fusion | flops 8388608 | bytes 34340864 | tf_op jit(solution)/shard_map/while/body/eval_jaxpr/mul | solution.py:111
  282.2 74.0 %while.209 = (s32[]{:T(128)}, f32[64,512]{1,0:T(8,128)S(1)}, f32[8,16,64,512]{3,1,2,0:T(8,128)}, f32[8,16,64,512]{3,1,2,0:T(8,128)}, f32[8,16,64,512]{3,1,2,0:T(8,128)}, /*index=5*/s32[]{:T(128)}) while((s32[]{:T(128)}, f32[64,512]{1,0:T(8,128)S(1)}, f32[8,16,64,512]{3,1,2,0:T(8,128)}, ...), condition=%wide.region_12.13_spmd.clone.clone, body=%wide.region_11.12_spmd.clone.clone.sunk | while | flops 203424768 | bytes 15337029 | solution.py:69
  356.3 15.4 %copy.49 = f32[8,16,64,512]{3,2,1,0:T(8,128)S(1)} copy(f32[8,16,64,512]{3,1,2,0:T(8,128)} %get-tuple-element.1016) | data formatting | bytes 33554432 | tf_op jit(solution)/shard_map/while/body/eval_jaxpr/while | solution.py:69
  388.0 8.1 multiply_reduce_fusion.13
  407.4 7.9 broadcast.226.clone.3
  415.3 74.4 %while.210 = (s32[]{:T(128)}, f32[64,512]{1,0:T(8,128)S(1)}, f32[8,16,64,512]{3,1,2,0:T(8,128)}, f32[8,16,64,512]{3,1,2,0:T(8,128)}, f32[8,16,64,512]{3,1,2,0:T(8,128)}, /*index=5*/s32[]{:T(128)}) while((s32[]{:T(128)}, f32[64,512]{1,0:T(8,128)S(1)}, f32[8,16,64,512]{3,1,2,0:T(8,128)}, ...), condition=%wide.region_27.28_spmd.clone.clone, body=%wide.region_26.27_spmd.clone.clone.sunk | while | flops 203424768 | bytes 15337029 | solution.py:69
  489.8 9.0 broadcast_multiply_fusion.1
  522.6 84.2 %while.206 = (s32[]{:T(128)}, f32[64,512]{1,0:T(8,128)S(1)}, f32[8,16,64,512]{3,1,2,0:T(8,128)}, f32[8,16,64,512]{3,1,2,0:T(8,128)}, f32[8,16,64,512]{3,1,2,0:T(8,128)}, /*index=5*/s32[]{:T(128)}, s32[]{:T(128)}) while((s32[]{:T(128)}, f32[64,512]{1,0:T(8,128)S(1)}, f32[8,16,64,512]{3,1,2,0:T(8,128)}, ...), condition=%wide.region_22.23_spmd.clone, body=%wide.region_21.22_spmd.clone.sunk | while | flops 203490304 | bytes 15729761 | solution.py:69
  607.1 15.2 %multiply_reduce_fusion.4 = (f32[64,512]{1,0:T(8,128)S(1)}, f32[8,16,512]{2,1,0:T(8,128)S(1)}, f32[64,512]{1,0:T(8,128)}, f32[8,16,512]{2,1,0:T(8,128)S(1)}, f32[64,512]{1,0:T(8,128)}) fusion(f32[8,16,512]{2,1,0:T(8,128)S(1)} %bitcast.607, f32[8,16,64,512]{3,1,2,0:T(8,128)} %get-tuple-element.1019, f32[8,16,64,512]{3,1,2,0:T(8,128)} %get-tuple-element.1020, ...), kind=kLoop, calls=%fused_computation.142 | loop fusion | flops 54296576 | bytes 35520512 | tf_op jit(solution)/shard_map/while/body/eval_jaxpr/reduce_sum | solution.py:192
  632.8 8.0 broadcast_multiply_fusion
  643.7 8.4 all_gather.45
  664.2 84.4 %while.207 = (s32[]{:T(128)}, f32[64,512]{1,0:T(8,128)S(1)}, f32[8,16,64,512]{3,1,2,0:T(8,128)}, f32[8,16,64,512]{3,1,2,0:T(8,128)}, f32[8,16,64,512]{3,1,2,0:T(8,128)}, /*index=5*/s32[]{:T(128)}, s32[]{:T(128)}) while((s32[]{:T(128)}, f32[64,512]{1,0:T(8,128)S(1)}, f32[8,16,64,512]{3,1,2,0:T(8,128)}, ...), condition=%wide.region_35.36_spmd.clone, body=%wide.region_34.35_spmd.clone.sunk | while | flops 203490304 | bytes 15729761 | solution.py:69
  748.8 13.9 %multiply_reduce_fusion.5 = (f32[64,512]{1,0:T(8,128)S(1)}, f32[8,16,512]{2,1,0:T(8,128)S(1)}, f32[64,512]{1,0:T(8,128)S(1)}, f32[8,16,512]{2,1,0:T(8,128)S(1)}, f32[64,512]{1,0:T(8,128)S(1)}) fusion(f32[8,16,512]{2,1,0:T(8,128)S(1)} %bitcast.605, f32[8,16,64,512]{3,1,2,0:T(8,128)} %get-tuple-element.1022, f32[8,16,64,512]{3,1,2,0:T(8,128)} %get-tuple-element.1023, ...), kind=kLoop, calls=%fused_computation.143 | loop fusion | flops 54296576 | bytes 35520512 | tf_op jit(solution)/shard_map/while/body/eval_jaxpr/reduce_sum | solution.py:192
  776.3 42.6 %all-reduce.4 = (f32[2,512]{1,0:T(2,128)}, f32[2,512]{1,0:T(2,128)}, f32[2,512]{1,0:T(2,128)}, f32[2,512]{1,0:T(2,128)}, f32[2,1024]{1,0:T(2,128)}, /*index=5*/f32[2,3]{1,0:T(2,128)S(1)}, f32[]{:T(128)}) all-reduce(f32[2,512]{1,0:T(2,128)S(1)} %pad_maximum_fusion.13, ...), channel_id=1, replica_groups=mesh['seq'=4,'batch'=8] {'seq','batch'}, use_global_device_ids=true, to_apply=%region_46.47 | all-reduce | flops 6151 | bytes 49208 | tf_op jit(solution)/shard_map/psum | solution.py:283
  822.1 97.4 %all-reduce.8.cloned.1.call-done = (f32[2,64,512]{2,1,0:T(8,128)}, f32[2,64,512]{2,1,0:T(8,128)}, f32[2,64,512]{2,1,0:T(8,128)}, f32[2,512,1024]{2,1,0:T(8,128)}) async-done(((f32[2,64,512]{2,1,0:T(8,128)}, f32[2,64,512]{2,1,0:T(8,128)}, f32[2,64,512]{2,1,0:T(8,128)}, f32[2,512,1024]{2,1,0:T(8,128)}), (f32[2,64,512]{2,1,0:T(8,128)}, f32[2,64,512]{2,1,0:T(8,128)}, f32[2,64,512]{2,1,0:T(8,128)}, ...) | async-done | bytes 4980752 | tf_op jit(solution)/shard_map/psum | solution.py:283
  (512 shorter events, 619.6 us)
Async XLA Ops:
  7.2 912.3 %all-reduce.8.cloned.1.call-start = ((), (), s32[]{:S(2)}) async-start(), calls=%async_computation | async-start | bytes 9961472 | tf_op jit(solution)/shard_map/psum | solution.py:283
  11.0 32.7 %copy-start.53 = (f32[1,512]{1,0:T(1,128)}, f32[1,512]{1,0:T(1,128)S(1)}, u32[]{:S(2)}) copy-start(f32[1,512]{1,0:T(1,128)S(1)} %get-tuple-element.1519) | copy-start | bytes 6148
  12.8 31.0 %copy-start.2 = (f32[1,128,512]{2,1,0:T(8,128)}, f32[1,128,512]{2,1,0:T(8,128)S(1)}, u32[]{:S(2)}) copy-start(f32[1,128,512]{2,1,0:T(8,128)S(1)} %get-tuple-element.1458) | copy-start | bytes 786436
  12.8 13.3 %collective-permute-start = (f32[1,512]{1,0:T(1,128)S(1)}, f32[1,512]{1,0:T(1,128)S(1)}, u32[]{:S(2)}, u32[]{:S(2)}) collective-permute-start(f32[1,512]{1,0:T(1,128)S(1)} %slice_bitcast_fusion.9), channel_id=1, source_target_pairs={{0,8},{8,16},{16,24},{1,9},{9,17},{17,25},{2,10},{10,18},{18,26},{... | collective-permute-start | bytes 6152 | tf_op jit(solution)/shard_map/ppermute | solution.py:15
  17.2 26.5 %copy-start.55 = (f32[1,512]{1,0:T(1,128)}, f32[1,512]{1,0:T(1,128)S(1)}, u32[]{:S(2)}) copy-start(f32[1,512]{1,0:T(1,128)S(1)} %get-tuple-element.1515) | copy-start | bytes 6148
  18.2 25.5 %copy-start.26 = (f32[64,512]{1,0:T(8,128)}, f32[64,512]{1,0:T(8,128)S(1)}, u32[]{:S(2)}) copy-start(f32[64,512]{1,0:T(8,128)S(1)} %get-tuple-element.1505) | copy-start | bytes 393220
  18.3 244.2 %copy-start.29 = (f32[64,512]{1,0:T(8,128)}, f32[64,512]{1,0:T(8,128)S(1)}, u32[]{:S(2)}) copy-start(f32[64,512]{1,0:T(8,128)S(1)} %get-tuple-element.1504) | copy-start | bytes 393220
  19.3 147.1 %copy-start.27 = (f32[64,512]{1,0:T(8,128)}, f32[64,512]{1,0:T(8,128)S(1)}, u32[]{:S(2)}) copy-start(f32[64,512]{1,0:T(8,128)S(1)} %get-tuple-element.1498) | copy-start | bytes 393220
  19.4 376.8 %copy-start.30 = (f32[64,512]{1,0:T(8,128)}, f32[64,512]{1,0:T(8,128)S(1)}, u32[]{:S(2)}) copy-start(f32[64,512]{1,0:T(8,128)S(1)} %get-tuple-element.1497) | copy-start | bytes 393220
  20.7 150.6 %copy-start.59 = (f32[1,512]{1,0:T(1,128)}, f32[1,512]{1,0:T(1,128)S(1)}, u32[]{:S(2)}) copy-start(f32[1,512]{1,0:T(1,128)S(1)} %get-tuple-element.1513) | copy-start | bytes 6148
  26.3 145.0 %copy-start.7 = (f32[1,128,512]{2,1,0:T(8,128)}, f32[1,128,512]{2,1,0:T(8,128)S(1)}, u32[]{:S(2)}) copy-start(f32[1,128,512]{2,1,0:T(8,128)S(1)} %get-tuple-element.1508) | copy-start | bytes 786436
  26.6 139.9 %copy-start.43 = (f32[1,128,512]{2,1,0:T(8,128)}, f32[1,128,512]{2,1,0:T(8,128)S(1)}, u32[]{:S(2)}) copy-start(f32[1,128,512]{2,1,0:T(8,128)S(1)} %reduce_window_sum.17) | copy-start | bytes 786436
  27.7 138.7 %copy-start.47 = (f32[64,512]{1,0:T(8,128)}, f32[64,512]{1,0:T(8,128)S(1)}, u32[]{:S(2)}) copy-start(f32[64,512]{1,0:T(8,128)S(1)} %get-tuple-element.1500) | copy-start | bytes 393220
  27.7 368.4 %copy-start.49 = (f32[64,512]{1,0:T(8,128)}, f32[64,512]{1,0:T(8,128)S(1)}, u32[]{:S(2)}) copy-start(f32[64,512]{1,0:T(8,128)S(1)} %get-tuple-element.1499) | copy-start | bytes 393220
  141.3 31.8 %copy-start.4 = (f32[1,128,512]{2,1,0:T(8,128)S(1)}, f32[1,128,512]{2,1,0:T(8,128)}, u32[]{:S(2)}) copy-start(f32[1,128,512]{2,1,0:T(8,128)} %param.32) | copy-start | bytes 786436
  175.5 86.7 %collective-permute-start.1 = (f32[1,512]{1,0:T(1,128)S(1)}, f32[1,512]{1,0:T(1,128)S(1)}, u32[]{:S(2)}, u32[]{:S(2)}) collective-permute-start(f32[1,512]{1,0:T(1,128)S(1)} %slice_bitcast_fusion.8), channel_id=1, source_target_pairs={{0,8},{8,16},{16,24},{1,9},{9,17},{17,25},{2,10},{10,18},{18,26},{... | collective-permute-start | bytes 6152 | tf_op jit(solution)/shard_map/ppermute | solution.py:15
  415.3 74.5 %copy-start.31 = (f32[64,512]{1,0:T(8,128)S(1)}, f32[64,512]{1,0:T(8,128)}, u32[]{:S(2)}) copy-start(f32[64,512]{1,0:T(8,128)} %copy-done.30) | copy-start | bytes 393220
  607.1 25.7 %copy-start.28 = (f32[64,512]{1,0:T(8,128)S(1)}, f32[64,512]{1,0:T(8,128)}, u32[]{:S(2)}) copy-start(f32[64,512]{1,0:T(8,128)} %copy-done.27) | copy-start | bytes 393220
  623.3 3.1 collective-permute-start.2
  664.2 84.4 %copy-start.8 = (f32[1,128,512]{2,1,0:T(8,128)S(1)}, f32[1,128,512]{2,1,0:T(8,128)}, u32[]{:S(2)}) copy-start(f32[1,128,512]{2,1,0:T(8,128)} %copy-done.7) | copy-start | bytes 786436
  664.2 84.4 %copy-start.10 = (f32[1,128,512]{2,1,0:T(8,128)S(1)}, f32[1,128,512]{2,1,0:T(8,128)}, u32[]{:S(2)}) copy-start(f32[1,128,512]{2,1,0:T(8,128)} %copy-done.9) | copy-start | bytes 786436
  664.2 84.4 %copy-start.25 = (f32[64,512]{1,0:T(8,128)S(1)}, f32[64,512]{1,0:T(8,128)}, u32[]{:S(2)}) copy-start(f32[64,512]{1,0:T(8,128)} %copy-done.24) | copy-start | bytes 393220
  762.7 56.8 %copy-start.82 = (f32[128]{0:T(128)S(1)}, f32[128]{0:T(128)}, u32[]{:S(2)}) copy-start(f32[128]{0:T(128)} %copy-done.81) | copy-start | bytes 1540
  763.5 12.3 %collective-permute-start.3 = (f32[1,512]{1,0:T(1,128)S(1)}, f32[1,512]{1,0:T(1,128)S(1)}, u32[]{:S(2)}, u32[]{:S(2)}) collective-permute-start(f32[1,512]{1,0:T(1,128)S(1)} %fusion.163), channel_id=1, source_target_pairs={{8,0},{16,8},{24,16},{9,1},{17,9},{25,17},{10,2},{18,10},{26,18},{... | collective-permute-start | bytes 6152 | tf_op jit(solution)/shard_map/ppermute | solution.py:15
  (67 other events, 975.7 us)
Sparse Core Ops, SparseCore 0:
  769.6 149.8 all-reduce.7
where the time goes:
time: 946 us; the launch traced here: 936 us
  matrix products  445 us (47%)
  other arithmetic  147 us (16%)
  local copies, waits for them, and re-layouts  127 us (13%)
  waiting for transfers between devices  97.8 us (10%)
  blocking collectives  89.3 us (9%)
  between operations  19.7 us (2%)
    dot_general x48, matrix products, one_block(): jnp.einsum('ts,snc->tnc', gathering, jnp.exp(accrued) * drive_block, prec...  261 us
    dot_general x48, matrix products, one_block(): accrued = jnp.einsum('ts,snc->tnc', leading, log_block, precision=highest)  176 us
    psum x1, waiting for transfers between devices, per_device(): lax.psum((stacked[0], stacked[1], stacked[2], stacked[3], stacked[4], sta...  97.4 us
    another operation x8, local copies, waits for them, and re-layouts  47.4 us
    all_gather x6, blocking collectives, prefix(): pieces = jax.tree.map(lambda part: lax.all_gather(part, axis), value)  46.7 us
    psum x1, blocking collectives, per_device(): lax.psum((stacked[0], stacked[1], stacked[2], stacked[3], stacked[4], sta...  42.6 us
    while x2, local copies, waits for them, and re-layouts, states_scan(): lax.scan(one_block, start, (logs_blocks, drive_blocks), reverse=reverse)  30.6 us
    reduce_sum x2, other arithmetic, review_back(): grad_rate_part = -jnp.sum(decay_term * rates_seq[:, None, :], axis=0)  29 us
  transfers between devices with their start and end apart: 5, of which 2 were waited for; matrix products, arithmetic and copies ran while one was open for 11% of the time, Pallas kernels for 0%

commit v1 on v0

v1 whole, which is shorter than its diff:
```python
import functools
import math

import jax
import jax.numpy as jnp
from jax import lax
from jax.experimental import pallas as pl
from jax.experimental.pallas import tpu as pltpu
from jax.sharding import PartitionSpec as P

MESH = pl.DeviceIdType.MESH
EPSILON = 1e-05
LOG2E = 1.4426950408889634
LN2 = 0.6931471805599453
GELU_K = math.sqrt(2.0 / math.pi)
F32 = jnp.float32
BF16 = jnp.bfloat16
LANES = 128
CHUNK = 32
EXTRA = 16


def rows8(v):
    return v.reshape(v.shape[0] // 8, 8, v.shape[1]).sum(0)


def sigmoid(v):
    return 1.0 / (1.0 + jnp.exp(-v))


def gelu_parts(m):
    th = jnp.tanh(GELU_K * (m + 0.044715 * m * m * m))
    return th


def bits_of(n):
    return [i for i in range(n.bit_length() - 1)]


def orders(seq, batch):
    s = [("seq", b) for b in bits_of(seq)]
    b = [("batch", b) for b in bits_of(batch)]
    first = s[:1]
    s, b = s[1:], b
    one, two = [], []
    for i in range(max(len(s), len(b))):
        one += s[i : i + 1] + b[i : i + 1]
        two += b[i : i + 1] + s[i : i + 1]
    return [first + one, first + two]


def kernel(cfg, *refs):
    S, B, TL, D, NS, L, UN = cfg
    CG = D // LANES
    NSP = S // CG
    NL = NS // NSP
    E2 = 2 * D
    CB = E2 // LANES
    GROWS = D * CB
    SB_ROWS = 2 * NL + 24
    plans = orders(S, B)
    HALF = GROWS // 2
    (
        x_ref, ct_ref, len_ref, gain_ref, dec_hbm, in_hbm, out_hbm, skip_ref, o2_ref, step_ref, w_hbm, bias_ref,
        y_out, gx_out, ggain_out, gdec_out, gin_out, gout_out, gskip_out, go2_out, gstep_out, gw_hbm, gbias_out, stats_out,
        W, DEC, INM, OUTM, NA, WT,
        XS, XR, RSTD, R, Y, YR, GS, GMR, GXR,
        SIG, P1, P2, LA, PJ, LG, GA, STR, GRD, ST,
        FB, RB, FG, SBW, SBR, SBG, VEC,
        load_sem, send_sem, recv_sem, ar_ssem, ar_rsem, sb_ssem, sb_rsem, sg_ssem, sg_rsem, out_sem,
    ) = refs
    U, GX = P2, Y
    me = lax.axis_index("seq")
    bi = lax.axis_index("batch")
    cg = me // NSP
    nh = lax.rem(me, NSP)
    n0 = nh * NL
    first_part = (nh == 0).astype(F32)
    clane = pl.ds(pl.multiple_of(cg * LANES, LANES), LANES)

    loads = [
        pltpu.make_async_copy(w_hbm, W, load_sem.at[0]),
        pltpu.make_async_copy(dec_hbm, DEC, load_sem.at[1]),
        pltpu.make_async_copy(in_hbm, INM, load_sem.at[2]),
        pltpu.make_async_copy(out_hbm, OUTM, load_sem.at[3]),
    ]
    for c in loads:
        c.start()

    barrier = pltpu.get_barrier_semaphore()
    partners = [(me ^ d, bi) for d in range(1, S)] + [(me, bi ^ (1 << b)) for b in bits_of(B)]
    for p in partners:
        pl.semaphore_signal(barrier, inc=1, device_id=p, device_id_type=MESH)

    pending = []

    def seq_copy(l, ph, j, src, dst):
        return pltpu.make_async_remote_copy(
            src_ref=src,
            dst_ref=dst,
            send_sem=send_sem.at[l * 4 + ph, j],
            recv_sem=recv_sem.at[l * 4 + ph, me],
            device_id=(j, bi),
            device_id_type=MESH,
        )

    def seq_wait(l, ph, k, src, dst):
        pltpu.make_async_remote_copy(
            src_ref=src,
            dst_ref=dst,
            send_sem=send_sem.at[l * 4 + ph, k],
            recv_sem=recv_sem.at[l * 4 + ph, k],
            device_id=(k, bi),
            device_id_type=MESH,
        ).wait_recv()

    def tblock(k):
        return pl.ds(pl.multiple_of(k * TL, TL), TL)

    def swap(axis, bit):
        return (me ^ (1 << bit), bi) if axis == "seq" else (me, bi ^ (1 << bit))

    def my_bit(axis, bit):
        return lax.rem((me if axis == "seq" else bi) // (1 << bit), 2)

    class Reduce:
        def __init__(self, l):
            self.l = l
            self.chains = []
            for c, plan in enumerate(plans):
                off, size, roff, stages = HALF * c, HALF, 0, []
                for i, (axis, bit) in enumerate(plan):
                    half = size // 2
                    mine = my_bit(axis, bit)
                    keep = pl.multiple_of(off + mine * half, 8)
                    give = pl.multiple_of(off + (1 - mine) * half, 8)
                    stages.append((i, axis, bit, half, keep, give, roff))
                    off, size, roff = keep, half, roff + half
                self.chains.append(stages)
            n = len(plans[0])
            self.n = n
            self.todo = [functools.partial(self.begin, 0)]
            for i in range(n):
                self.todo.append(functools.partial(self.reduce_step, i))
            for i in range(n - 1, -1, -1):
                self.todo.append(functools.partial(self.gather_step, i))

        def rs(self, c, stage):
            i, axis, bit, half, keep, give, roff = stage
            return pltpu.make_async_remote_copy(
                src_ref=FB.at[self.l, pl.ds(give, half)],
                dst_ref=RB.at[self.l, c, pl.ds(roff, half)],
                send_sem=ar_ssem.at[(self.l * 2 + c) * 2, i],
                recv_sem=ar_rsem.at[(self.l * 2 + c) * 2, i],
                device_id=swap(axis, bit),
                device_id_type=MESH,
            )

        def ag(self, c, stage):
            i, axis, bit, half, keep, give, roff = stage
            return pltpu.make_async_remote_copy(
                src_ref=FG.at[self.l, pl.ds(keep, half)],
                dst_ref=FG.at[self.l, pl.ds(keep, half)],
                send_sem=ar_ssem.at[(self.l * 2 + c) * 2 + 1, i],
                recv_sem=ar_rsem.at[(self.l * 2 + c) * 2 + 1, i],
                device_id=swap(axis, bit),
                device_id_type=MESH,
            )

        def begin(self, i):
            for c, stages in enumerate(self.chains):
                self.rs(c, stages[i]).start()

        def reduce_step(self, i):
            for c, stages in enumerate(self.chains):
                _, _, _, half, keep, _, roff = stages[i]
                self.rs(c, stages[i]).wait()
                step = min(half, 64)
                total = FB if i + 1 < self.n else FG

                def add(j, _, keep=keep, roff=roff, step=step, total=total):
                    at = pl.ds(pl.multiple_of(keep + j * step, 8), step)
                    total[self.l, at, :] = FB[self.l, at, :] + RB[self.l, c, pl.ds(pl.multiple_of(roff + j * step, 8), step), :]
                    return 0

                lax.fori_loop(0, half // step, add, 0)
                if i + 1 < self.n:
                    self.rs(c, stages[i + 1]).start()
                else:
                    self.ag(c, stages[i]).start()

        def gather_step(self, i):
            for c, stages in enumerate(self.chains):
                self.ag(c, stages[i]).wait()
                if i > 0:
                    self.ag(c, stages[i - 1]).start()
                else:
                    for q in range(CB // 2):
                        cb = c * (CB // 2) + q
                        copy = pltpu.make_async_copy(
                            FG.at[self.l, pl.ds(cb * D, D)],
                            gw_hbm.at[self.l, :, pl.ds(cb * LANES, LANES)],
                            out_sem.at[self.l, cb],
                        )
                        copy.start()
                        pending.append(copy.wait)

        def tick(self):
            if self.todo:
                self.todo.pop(0)()

    def norm_forward(l, src):
        def step(i, _):
            rows = pl.ds(pl.multiple_of(i * CHUNK, CHUNK), CHUNK)
            x = src[rows, :]
            center = x - jnp.mean(x, axis=-1, keepdims=True)
            spread = jnp.mean(center * center, axis=-1, keepdims=True)
            inv = lax.rsqrt(spread + EPSILON)
            xhat = center * inv
            RSTD[l, rows, :] = jnp.broadcast_to(inv, (CHUNK, LANES))
            for g in range(CG):
                XS[l, g, rows, :] = xhat[:, g * LANES : (g + 1) * LANES]
            return 0

        lax.fori_loop(0, TL // CHUNK, step, 0)

    def send_normed(l):
        for d in range(1, S):
            j = me ^ d
            copy = seq_copy(l, 0, j, XS.at[l, j // NSP], XR.at[l, tblock(me)])
            copy.start()
            pending.append(copy.wait_send)
        XR[l, tblock(me), :] = XS[l, cg]

    def scan_forward(l):
        gain = gain_ref[l : l + 1, clane]
        o2 = o2_ref[l : l + 1, clane]
        stp = step_ref[l : l + 1, clane]
        skip = skip_ref[l : l + 1, clane] * first_part
        first_row = lax.broadcasted_iota(jnp.int32, (TL, LANES), 0) == 0
        SIG[l, 0] = jnp.zeros((NL, LANES), F32)

        def block(k, carry):
            sig, last = carry

            @pl.when(k != me)
            def _():
                seq_wait(l, 0, k, XS.at[l, 0], XR.at[l, tblock(k)])

            normed = XR[l, tblock(k), :] * gain
            prev = jnp.where(first_row, last, pltpu.roll(normed, 1, 0))
            U[tblock(k), :] = normed + o2 * normed * prev
            z = stp * normed
            R[l, tblock(k), :] = jnp.maximum(z, 0.0) + jnp.log1p(jnp.exp(-jnp.abs(z)))
            na, wt = NA[l], WT[l]

            def inner(i, sig):
                for s in range(UN):
                    t = i * UN + s
                    at = pl.ds(k * TL + t, 1)
                    sig = jnp.exp2(na * R[l, at, :]) * sig + U[at, :]
                    SIG[l, k * TL + t + 1] = sig
                    P1[pl.ds(pl.multiple_of(t * 8, 8), 8), :] = rows8(wt * sig)
                return sig

            sig = lax.fori_loop(0, TL // UN, inner, sig)

            def finish(j, _):
                total = P1[pl.ds(j * 64, 8, stride=8), :]
                for s in range(1, 8):
                    total = total + P1[pl.ds(j * 64 + s, 8, stride=8), :]
                at = pl.ds(pl.multiple_of(k * TL + j * 8, 8), 8)
                Y[at, :] = total + skip * U[at, :]
                return 0

            lax.fori_loop(0, TL // 8, finish, 0)

            @pl.when(k == me)
            def _():
                YR[l, me] = Y[tblock(k), :]

            @pl.when(k != me)
            def _():
                seq_copy(l, 1, k, Y.at[tblock(k)], YR.at[l, me]).start()

            return sig, normed[TL - 1 : TL, :]

        lax.fori_loop(0, S, block, (jnp.zeros((NL, LANES), F32), jnp.zeros((1, LANES), F32)))
        return [seq_copy(l, 1, me ^ d, Y.at[tblock(me ^ d)], YR.at[l, me]).wait_send for d in range(1, S)]

    def mixed_of(l, g, rows):
        m = YR[l, g * NSP, rows, :]
        for h in range(1, NSP):
            m = m + YR[l, g * NSP + h, rows, :]
        return m

    def valid_of(i):
        pos = me * TL + i * CHUNK + lax.broadcasted_iota(jnp.int32, (CHUNK, 1), 0)
        return (pos < len_ref[0]).astype(F32)

    def glu_forward(l, src, dst):
        for d in range(1, S):
            j = me ^ d
            seq_wait(l, 1, j, Y.at[pl.ds(0, TL)], YR.at[l, j])

        def act(i, sq):
            rows = pl.ds(pl.multiple_of(i * CHUNK, CHUNK), CHUNK)
            valid = valid_of(i)
            for g in range(CG):
                m = mixed_of(l, g, rows)
                a = 0.5 * m * (1.0 + gelu_parts(m))
                LA[l, rows, g * LANES : (g + 1) * LANES] = a.astype(BF16)
                sq = sq + rows8(a * a * valid)
            return sq

        zero = jnp.zeros((8, LANES), F32)
        sq_act = lax.fori_loop(0, TL // CHUNK, act, zero)
        PJ[l] = jnp.dot(LA[l], W[l], preferred_element_type=F32) + bias_ref[l : l + 1, :]

        def gate(i, sq):
            sq_b, sq_s, cnt = sq
            rows = pl.ds(pl.multiple_of(i * CHUNK, CHUNK), CHUNK)
            valid = valid_of(i)
            for g in range(CG):
                cols = slice(g * LANES, (g + 1) * LANES)
                gcols = slice(D + g * LANES, D + (g + 1) * LANES)
                branch = PJ[l, rows, cols] * sigmoid(PJ[l, rows, gcols]) * valid
                out = src[rows, cols] + branch
                dst[rows, cols] = out
                sq_b = sq_b + rows8(branch * branch)
                sq_s = sq_s + rows8(out * out * valid)
            cnt = cnt + rows8(jnp.broadcast_to(valid, (CHUNK, LANES)))
            return sq_b, sq_s, cnt

        sq_b, sq_s, cnt = lax.fori_loop(0, TL // CHUNK, gate, (zero, zero, zero))
        for k, v in enumerate((sq_act, sq_b, sq_s, cnt)):
            ST[l, k] = v

    def glu_backward(l, gsrc):
        def gate(i, acc):
            rows = pl.ds(pl.multiple_of(i * CHUNK, CHUNK), CHUNK)
            valid = valid_of(i)
            out = []
            for g in range(CG):
                cols = slice(g * LANES, (g + 1) * LANES)
                gcols = slice(D + g * LANES, D + (g + 1) * LANES)
                gb = gsrc[rows, cols] * valid
                s = sigmoid(PJ[l, rows, gcols])
                one = gb * s
                two = one * PJ[l, rows, cols] * (1.0 - s)
                LG[rows, cols] = one.astype(BF16)
                LG[rows, gcols] = two.astype(BF16)
                out.append((rows8(one), rows8(two)))
            return tuple(a + b for a, b in zip(acc, [o[0] for o in out] + [o[1] for o in out]))

        zero = jnp.zeros((8, LANES), F32)
        bias = lax.fori_loop(0, TL // CHUNK, gate, (zero,) * CB)
        GA[...] = lax.dot_general(LG[...], W[l], (((1,), (1,)), ((), ())), preferred_element_type=F32)

        def act(i, _):
            rows = pl.ds(pl.multiple_of(i * CHUNK, CHUNK), CHUNK)
            for g in range(CG):
                m = mixed_of(l, g, rows)
                th = gelu_parts(m)
                slope = 0.5 * (1.0 + th) + 0.5 * m * (1.0 - th * th) * GELU_K * (1.0 + 3 * 0.044715 * m * m)
                GS[l, g, rows, :] = GA[rows, g * LANES : (g + 1) * LANES] * slope
            return 0

        lax.fori_loop(0, TL // CHUNK, act, 0)
        extra = [jnp.sum(b, axis=0, keepdims=True) for b in bias]
        extra += [jnp.sum(ST[l, k], axis=0, keepdims=True) for k in range(4)]
        extra += [jnp.zeros((EXTRA - len(extra), LANES), F32)]
        extra = jnp.concatenate(extra, axis=0)
        for g in range(CG):
            GS[l, g, TL : TL + EXTRA, :] = extra
        for d in range(1, S):
            j = me ^ d
            copy = seq_copy(l, 2, j, GS.at[l, j // NSP], GMR.at[l, me])
            copy.start()
            pending.append(copy.wait_send)
        GMR[l, me] = GS[l, cg]

    def weight_grad(l):
        for c in range(2):
            half = lax.dot_general(
                LA[l], LG[:, c * D : (c + 1) * D], (((0,), (0,)), ((), ())), preferred_element_type=F32
            )
            for q in range(CB // 2):
                FB[l, pl.ds((c * (CB // 2) + q) * D, D), :] = half[:, q * LANES : (q + 1) * LANES]

    def scan_backward(l, ticks):
        gain = gain_ref[l : l + 1, clane]
        o2 = o2_ref[l : l + 1, clane]
        stp = step_ref[l : l + 1, clane]
        skip = skip_ref[l : l + 1, clane]
        row_id = lax.broadcasted_iota(jnp.int32, (TL, LANES), 0)
        zero8 = jnp.zeros((8, LANES), F32)
        zeros = jnp.zeros((NL, LANES), F32)
        for v in range(4):
            VEC[v] = zero8

        def block(kk, carry):
            nu, acc, gdc, after = carry
            k = S - 1 - kk

            @pl.when(k != me)
            def _():
                seq_wait(l, 2, k, GS.at[l, 0], GMR.at[l, k])

            na, wt = NA[l], WT[l]

            def inner(ii, c):
                nu, acc, gdc = c
                i = TL // UN - 1 - ii
                for s in range(UN - 1, -1, -1):
                    t = i * UN + s
                    rate = R[l, pl.ds(k * TL + t, 1), :]
                    gm = GMR[l, k, pl.ds(t, 1), :]
                    mu = wt * gm + nu
                    acc = acc + gm * SIG[l, k * TL + t + 1]
                    at = pl.ds(pl.multiple_of(t * 8, 8), 8)
                    P1[at, :] = rows8(mu)
                    nu = jnp.exp2(na * rate) * mu
                    q = nu * SIG[l, k * TL + t]
                    gdc = gdc + q * rate
                    P2[at, :] = rows8(na * q)
                return nu, acc, gdc

            nu, acc, gdc = lax.fori_loop(0, TL // UN, inner, (nu, acc, gdc))

            def finish(j, _):
                one = P1[pl.ds(j * 64, 8, stride=8), :]
                two = P2[pl.ds(j * 64, 8, stride=8), :]
                for s in range(1, 8):
                    one = one + P1[pl.ds(j * 64 + s, 8, stride=8), :]
                    two = two + P2[pl.ds(j * 64 + s, 8, stride=8), :]
                at = pl.ds(pl.multiple_of(j * 8, 8), 8)
                GX[pl.ds(pl.multiple_of(k * TL + j * 8, 8), 8), :] = one
                GA[at, 0:LANES] = two
                return 0

            lax.fori_loop(0, TL // 8, finish, 0)
            xhat = XR[l, tblock(k), :]
            normed = xhat * gain
            before = XR[l, pl.ds(jnp.maximum(k * TL - 1, 0), 1), :] * gain
            before = jnp.where(k == 0, 0.0, before)
            prev = jnp.where(row_id == 0, before, pltpu.roll(normed, 1, 0))
            gm = GMR[l, k, 0:TL, :] * first_part
            gdrv = GX[tblock(k), :] + skip * gm
            grate = GA[0:TL, 0:LANES] * LN2
            both = gdrv * normed
            h = o2 * both
            later = jnp.where(row_id == TL - 1, after, pltpu.roll(h, TL - 1, 0))
            slope = sigmoid(stp * normed) * grate
            gnormed = gdrv * (1.0 + o2 * prev) + later + slope * stp
            GX[tblock(k), :] = gnormed * gain
            VEC[0] = VEC[0] + rows8(gm * (normed + o2 * normed * prev))
            VEC[1] = VEC[1] + rows8(both * prev)
            VEC[2] = VEC[2] + rows8(slope * normed)
            VEC[3] = VEC[3] + rows8(gnormed * xhat)

            @pl.when(k == me)
            def _():
                GXR[l, me] = GX[tblock(k), :]

            @pl.when(k != me)
            def _():
                seq_copy(l, 3, k, GX.at[tblock(k)], GXR.at[l, me]).start()

            for at, tick in ticks.items():

                @pl.when(kk == at)
                def _(tick=tick):
                    tick()

            return nu, acc, gdc, h[0:1, :]

        carry = (zeros, zeros, zeros, jnp.zeros((1, LANES), F32))
        _, acc, gdc, _ = lax.fori_loop(0, S, block, carry)
        sent = [seq_copy(l, 3, me ^ d, GX.at[tblock(me ^ d)], GXR.at[l, me]).wait_send for d in range(1, S)]
        SBW[l, 0, 0:NL, :] = acc
        SBW[l, 0, NL : 2 * NL, :] = gdc
        vec = [jnp.sum(VEC[v], axis=0, keepdims=True) for v in range(4)]
        vec += [jnp.zeros((4, LANES), F32)]
        SBW[l, 0, 2 * NL : 2 * NL + 8, :] = jnp.concatenate(vec, axis=0)
        extra = GMR[l, 0, TL : TL + EXTRA, :]
        for k in range(1, S):
            extra = extra + GMR[l, k, TL : TL + EXTRA, :]
        SBW[l, 0, 2 * NL + 8 : 2 * NL + 8 + EXTRA, :] = extra
        return sent

    class Small:
        def __init__(self, l):
            self.l = l
            nb = len(bits_of(B))
            self.todo = [functools.partial(self.start, 0)]
            self.todo += [functools.partial(self.join, i) for i in range(nb)]
            self.todo += [self.gathered]
            self.nb = nb

        def copy(self, i):
            return pltpu.make_async_remote_copy(
                src_ref=SBW.at[self.l, i],
                dst_ref=SBR.at[self.l, i],
                send_sem=sb_ssem.at[self.l, i],
                recv_sem=sb_rsem.at[self.l, i],
                device_id=(me, bi ^ (1 << i)),
                device_id_type=MESH,
            )

        def seq(self, j, slot, rslot):
            return pltpu.make_async_remote_copy(
                src_ref=SBW.at[self.l, self.nb],
                dst_ref=SBG.at[self.l, slot],
                send_sem=sg_ssem.at[self.l, j],
                recv_sem=sg_rsem.at[self.l, rslot],
                device_id=(j, bi),
                device_id_type=MESH,
            )

        def start(self, i):
            self.copy(i).start()

        def join(self, i):
            self.copy(i).wait()
            SBW[self.l, i + 1] = SBW[self.l, i] + SBR[self.l, i]
            if i + 1 < self.nb:
                self.start(i + 1)
            else:
                for d in range(1, S):
                    self.seq(me ^ d, me, me).start()
                SBG[self.l, me] = SBW[self.l, self.nb]

        def gathered(self):
            for d in range(1, S):
                self.seq(me ^ d, me ^ d, me ^ d).wait()
            l = self.l
            for g in range(CG):
                cols = slice(g * LANES, (g + 1) * LANES)
                vec = None
                for h in range(NSP):
                    slot = g * NSP + h
                    rows = slice(h * NL, (h + 1) * NL)
                    acc = SBG[l, slot, 0:NL, :]
                    gin_out[l, rows, cols] = OUTM[l, rows, cols] * acc
                    gout_out[l, rows, cols] = INM[l, rows, cols] * acc
                    gdec_out[l, rows, cols] = -SBG[l, slot, NL : 2 * NL, :]
                    part = SBG[l, slot, 2 * NL : 2 * NL + 8, :]
                    vec = part if vec is None else vec + part
                gskip_out[l : l + 1, cols] = vec[0:1]
                go2_out[l : l + 1, cols] = vec[1:2]
                gstep_out[l : l + 1, cols] = vec[2:3]
                ggain_out[l : l + 1, cols] = vec[3:4]
            base = 2 * NL + 8
            for q in range(CB):
                gbias_out[l : l + 1, q * LANES : (q + 1) * LANES] = SBG[l, 0, base + q : base + q + 1, :]
            sq = jnp.sum(SBG[l, 0, base + CB : base + CB + 8, :], axis=1, keepdims=True)
            count = sq[3:4] * (1.0 / LANES)
            root = jnp.sqrt(sq[0:3] / (count * D))
            col = lax.broadcasted_iota(jnp.int32, (1, 3), 1)
            stats_out[l : l + 1, :] = jnp.where(col == 0, root[0:1], jnp.where(col == 1, root[1:2], root[2:3]))

        def tick(self):
            if self.todo:
                self.todo.pop(0)()

    def norm_backward(l, gsrc, gdst):
        for d in range(1, S):
            j = me ^ d
            seq_wait(l, 3, j, GX.at[pl.ds(0, TL)], GXR.at[l, j])

        def step(i, _):
            rows = pl.ds(pl.multiple_of(i * CHUNK, CHUNK), CHUNK)
            inv = RSTD[l, rows, :]
            gx, xh = [], []
            s1 = s2 = None
            for g in range(CG):
                v = GXR[l, g * NSP, rows, :]
                for h in range(1, NSP):
                    v = v + GXR[l, g * NSP + h, rows, :]
                x = XS[l, g, rows, :]
                gx.append(v)
                xh.append(x)
                s1 = v if s1 is None else s1 + v
                s2 = v * x if s2 is None else s2 + v * x
            m1 = jnp.sum(s1, axis=-1, keepdims=True) * (1.0 / D)
            m2 = jnp.sum(s2, axis=-1, keepdims=True) * (1.0 / D)
            for g in range(CG):
                cols = slice(g * LANES, (g + 1) * LANES)
                gdst[rows, cols] = gsrc[rows, cols] + inv * (gx[g] - m1 - xh[g] * m2)
            return 0

        lax.fori_loop(0, TL // CHUNK, step, 0)

    norm_forward(0, x_ref)
    pl.semaphore_wait(barrier, len(partners))
    send_normed(0)
    for c in loads:
        c.wait()
    nrows = pl.ds(pl.multiple_of(n0, 8), NL)
    for l in range(L):
        NA[l] = DEC[l, nrows, clane] * (-LOG2E)
        WT[l] = INM[l, nrows, clane] * OUTM[l, nrows, clane]
    streams = [x_ref] + [STR.at[l] for l in range(L - 1)] + [y_out]
    for l in range(L):
        if l:
            norm_forward(l, streams[l])
            send_normed(l)
        sent = scan_forward(l)
        glu_forward(l, streams[l], streams[l + 1])
        for done in sent:
            done()

    grads = [gx_out] + [GRD.at[l] for l in range(L - 1)] + [ct_ref]
    reduces = []
    smalls = []
    for l in range(L - 1, -1, -1):
        glu_backward(l, grads[l + 1])
        weight_grad(l)
        mine = Reduce(l)
        mine.tick()
        reduces.append(mine)

        def some():
            for r in reduces + smalls:
                r.tick()

        ticks = {}
        if S >= 4:
            ticks = {S // 4 - 1: some, S // 2 - 1: some, 3 * S // 4 - 1: some}
        sent = scan_backward(l, ticks)
        small = Small(l)
        small.tick()
        smalls.append(small)
        some()
        norm_backward(l, grads[l + 1], grads[l])
        for done in sent:
            done()
    while any(r.todo for r in reduces + smalls):
        for r in reduces + smalls:
            r.tick()
    for done in pending:
        done()


def per_device(
    stream_in, cotangent, lengths, norm_gain, decay_rate, in_map, out_map, skip_gain, order_two, step_gain, glu_weight, glu_bias
):
    S, B = lax.axis_size("seq"), lax.axis_size("batch")
    _, TL, D = stream_in.shape
    L, NS = decay_rate.shape[:2]
    UN = math.gcd(TL, 16)
    CG, E2 = D // LANES, 2 * D
    NL = NS // (S // CG)
    TA = S * TL
    CB = E2 // LANES
    GROWS = D * CB
    SBR = 2 * NL + 8 + EXTRA
    NB, NST = len(bits_of(B)), len(bits_of(B)) + len(bits_of(S))
    shape = jax.ShapeDtypeStruct
    vmem = pl.BlockSpec(memory_space=pltpu.VMEM)
    smem = pl.BlockSpec(memory_space=pltpu.SMEM)
    hbm = pl.BlockSpec(memory_space=pl.ANY)
    buf = pltpu.VMEM
    dma = pltpu.SemaphoreType.DMA
    outs = pl.pallas_call(
        functools.partial(kernel, (S, B, TL, D, NS, L, UN)),
        out_shape=[
            shape((TL, D), F32), shape((TL, D), F32), shape((L, D), F32),
            shape((L, NS, D), F32), shape((L, NS, D), F32), shape((L, NS, D), F32),
            shape((L, D), F32), shape((L, D), F32), shape((L, D), F32),
            shape((L, D, E2), F32), shape((L, E2), F32), shape((L, 3), F32),
        ],
        in_specs=[vmem, vmem, smem, vmem, hbm, hbm, hbm, vmem, vmem, vmem, hbm, vmem],
        out_specs=[vmem] * 9 + [hbm, vmem, vmem],
        scratch_shapes=[
            buf((L, D, E2), BF16), buf((L, NS, D), F32), buf((L, NS, D), F32), buf((L, NS, D), F32),
            buf((L, NL, LANES), F32), buf((L, NL, LANES), F32),
            buf((L, CG, TL, LANES), F32), buf((L, TA, LANES), F32), buf((L, TL, LANES), F32),
            buf((L, TA, LANES), F32), buf((TA, LANES), F32),
            buf((L, S, TL, LANES), F32), buf((L, CG, TL + EXTRA, LANES), F32), buf((L, S, TL + EXTRA, LANES), F32),
            buf((L, S, TL, LANES), F32),
            buf((L, TA + 1, NL, LANES), F32), buf((TL * 8, LANES), F32), buf((max(TL * 8, TA), LANES), F32),
            buf((L, TL, D), BF16), buf((L, TL, E2), F32), buf((TL, E2), BF16), buf((TL, D), F32),
            buf((L - 1, TL, D), F32), buf((L - 1, TL, D), F32), buf((L, 4, 8, LANES), F32),
            buf((L, GROWS, LANES), F32), buf((L, 2, GROWS // 2, LANES), F32), buf((L, GROWS, LANES), F32),
            buf((L, NB + 1, SBR, LANES), F32), buf((L, NB, SBR, LANES), F32), buf((L, S, SBR, LANES), F32),
            buf((4, 8, LANES), F32),
            dma((4,)), dma((L * 4, S)), dma((L * 4, S)), dma((L * 4, NST)), dma((L * 4, NST)),
            dma((L, NB)), dma((L, NB)), dma((L, S)), dma((L, S)), dma((L, CB)),
        ],
        compiler_params=pltpu.CompilerParams(
            collective_id=0, has_side_effects=True, vmem_limit_bytes=61 * 2**20
        ),
        name="liquid_layers",
    )(
        stream_in[0], cotangent[0], lengths, norm_gain, decay_rate, in_map, out_map,
        skip_gain, order_two, step_gain, glu_weight, glu_bias,
    )
    return (outs[0][None], outs[1][None], *outs[2:])


def solution(mesh):
    split = P("batch", "seq", None)
    in_specs = (split, split, P("batch")) + (P(),) * 9
    out_specs = (split, split) + (P(),) * 10
    return jax.shard_map(per_device, mesh=mesh, in_specs=in_specs, out_specs=out_specs, check_vma=False)
```

time: 946 us -> 136 us (0.14)
  matrix products: 445 us -> 0 us
  other arithmetic: 147 us -> 0 us
  Pallas kernels: 0 us -> 115 us
  local copies, waits for them, and re-layouts: 127 us -> 19.4 us
  waiting for transfers between devices: 97.8 us -> 0 us
  blocking collectives: 89.3 us -> 0 us
  between operations: 19.7 us -> 1.31 us
    dot_general x102 -> x0, matrix products: 445 us -> none  [the longest x48 261 us: one_block(): jnp.einsum('ts,snc->tnc', gathering, jnp.exp(accrued) * drive_block, prec...]
    pallas_call x0 -> x1, Pallas kernels: none -> 115 us  [per_device(): pl.pallas_call(functools.partial(kernel, (S, B, TL, D, NS, L, UN)), out_s...]
    psum x1 -> x0, waiting for transfers between devices: 97.4 us -> none  [per_device(): lax.psum((stacked[0], stacked[1], stacked[2], stacked[3], stacked[4], sta...]
    reduce_sum x25 -> x0, other arithmetic: 72.4 us -> none  [the longest x2 29 us: review_back(): grad_rate_part = -jnp.sum(decay_term * rates_seq[:, None, :], axis=0)]
    mul x30 -> x0, other arithmetic: 50.2 us -> none  [the longest x2 19.9 us: local_pass(): in_map[None] * driven_seq[:, None, :]]
    another operation x8 -> x0, local copies, waits for them, and re-layouts: 47.4 us -> none
    all_gather x6 -> x0, blocking collectives: 46.7 us -> none  [prefix(): pieces = jax.tree.map(lambda part: lax.all_gather(part, axis), value)]
    psum x1 -> x0, blocking collectives: 42.6 us -> none  [per_device(): lax.psum((stacked[0], stacked[1], stacked[2], stacked[3], stacked[4], sta...]
  transfers between devices with their start and end apart: 5 -> 0, of which waited for: 2 -> 0; matrix products, arithmetic and copies ran while one was open for 11% -> 0% of each run, Pallas kernels for 0% -> 0%
where the time goes in v1:
time: 136 us
  Pallas kernels  115 us (85%)
  local copies, waits for them, and re-layouts  19.4 us (14%)
    pallas_call x1, Pallas kernels, per_device(): pl.pallas_call(functools.partial(kernel, (S, B, TL, D, NS, L, UN)), out_s...  115 us
    unnamed x16, local copies, waits for them, and re-layouts  19.4 us

profile of v1, /device:TPU:0, one launch (start us, length us, event | category | flops | bytes accessed | tf_op | source)
XLA Modules:
  0.0 135.5 jit_solution(5007774846151981155)
XLA Ops:
  1.3 114.8 %liquid_layers.1 = (f32[128,512]{1,0:T(8,128)}, f32[128,512]{1,0:T(8,128)}, f32[2,512]{1,0:T(2,128)}, f32[2,64,512]{2,1,0:T(8,128)}, f32[2,64,512]{2,1,0:T(8,128...) custom-call(f32[128,512]{1,0:T(8,128)} %bitcast.4, ...), custom_call_target="tpu_custom_call" | custom-call | tf_op jit(solution)/shard_map/liquid_layers/pallas_call | solution.py:666
  116.1 1.7 %copy.37 = f32[1,128,512]{2,1,0:T(8,128)} copy(f32[1,128,512]{2,1,0:T(8,128)} %bitcast.7) | data formatting | bytes 524288
  117.8 1.7 %copy.38 = f32[1,128,512]{2,1,0:T(8,128)} copy(f32[1,128,512]{2,1,0:T(8,128)} %bitcast.6) | data formatting | bytes 524288
  119.5 1.3 copy.39
  120.7 1.7 %copy.40 = f32[2,64,512]{2,1,0:T(8,128)} copy(f32[2,64,512]{2,1,0:T(8,128)} %get-tuple-element.51) | data formatting | bytes 524288
  122.4 1.7 %copy.41 = f32[2,64,512]{2,1,0:T(8,128)} copy(f32[2,64,512]{2,1,0:T(8,128)} %get-tuple-element.52) | data formatting | bytes 524288
  124.1 1.7 %copy.42 = f32[2,64,512]{2,1,0:T(8,128)} copy(f32[2,64,512]{2,1,0:T(8,128)} %get-tuple-element.53) | data formatting | bytes 524288
  125.7 1.3 copy.43
  127.0 1.3 copy.44
  128.3 1.3 copy.45
  129.6 0.0 copy-start
  129.6 0.0 copy-start.1
  129.6 4.8 %copy.46 = f32[2,512,1024]{2,1,0:T(8,128)} copy(f32[2,512,1024]{2,1,0:T(8,128)} %get-tuple-element.57) | data formatting | bytes 8388608
  134.4 0.0 copy-done
  134.4 0.6 copy.47
  135.0 0.0 copy-done.1
  135.0 0.6 copy.48
Async XLA Ops:
  129.6 4.8 %copy-start = (f32[2,1024]{1,0:T(2,128)S(1)}, f32[2,1024]{1,0:T(2,128)}, u32[]{:S(2)}) copy-start(f32[2,1024]{1,0:T(2,128)} %get-tuple-element.58) | copy-start | bytes 24580
  129.6 5.4 %copy-start.1 = (f32[2,3]{1,0:T(2,128)S(1)}, f32[2,3]{1,0:T(2,128)}, u32[]{:S(2)}) copy-start(f32[2,3]{1,0:T(2,128)} %get-tuple-element.59) | copy-start | bytes 76

commit v2 on v1

--- a/solution.py
+++ b/solution.py
@@ -641,6 +641,24 @@
             r.tick()
     for done in pending:
         done()
+
+
+def hand_on(n, *refs):
+    ins, outs, held, sem_in, sem_out = refs[:n], refs[n : 2 * n], refs[2 * n : 3 * n], refs[-2], refs[-1]
+    parts = []
+    for a, o, h in zip(ins, outs, held):
+        if len(a.shape) == 3:
+            parts += [(a.at[l], h.at[l], o.at[l]) for l in range(a.shape[0])]
+        else:
+            parts.append((a, h, o))
+    parts.sort(key=lambda p: math.prod(p[0].shape))
+    for i, (a, h, _) in enumerate(parts):
+        pltpu.make_async_copy(a, h, sem_in.at[i]).start()
+    for i, (a, h, o) in enumerate(parts):
+        pltpu.make_async_copy(a, h, sem_in.at[i]).wait()
+        pltpu.make_async_copy(h, o, sem_out.at[i]).start()
+    for i, (_, h, o) in enumerate(parts):
+        pltpu.make_async_copy(h, o, sem_out.at[i]).wait()
 
 
 def per_device(
@@ -697,6 +715,15 @@
         stream_in[0], cotangent[0], lengths, norm_gain, decay_rate, in_map, out_map,
         skip_gain, order_two, step_gain, glu_weight, glu_bias,
     )
+    outs = pl.pallas_call(
+        functools.partial(hand_on, len(outs)),
+        out_shape=[shape(o.shape, o.dtype) for o in outs],
+        in_specs=[hbm] * len(outs),
+        out_specs=[hbm] * len(outs),
+        scratch_shapes=[buf(o.shape, o.dtype) for o in outs] + [dma((2 * len(outs),)), dma((2 * len(outs),))],
+        compiler_params=pltpu.CompilerParams(vmem_limit_bytes=61 * 2**20),
+        name="results",
+    )(*outs)
     return (outs[0][None], outs[1][None], *outs[2:])
 
 

time: 136 us -> 121 us (0.89)
  local copies, waits for them, and re-layouts: 19.4 us -> 0 us
  Pallas kernels: 115 us -> 120 us
    unnamed x16 -> x0, local copies, waits for them, and re-layouts: 19.4 us -> none
    pallas_call x0 -> x1, Pallas kernels: none -> 5.07 us  [per_device(): pl.pallas_call(functools.partial(hand_on, len(outs)), out_shape=[shape(o....]
where the time goes in v2:
time: 121 us
  Pallas kernels  120 us (99%)
  between operations  1.3 us (1%)
    pallas_call x1, Pallas kernels, per_device(): pl.pallas_call(functools.partial(kernel, (S, B, TL, D, NS, L, UN)), out_s...  115 us
    pallas_call x1, Pallas kernels, per_device(): pl.pallas_call(functools.partial(hand_on, len(outs)), out_shape=[shape(o....  5.07 us

profile of v2, /device:TPU:0, one launch (start us, length us, event | category | flops | bytes accessed | tf_op | source)
XLA Modules:
  0.0 121.2 jit_solution(9244885255841491664)
XLA Ops:
  1.3 114.8 %liquid_layers.1 = (f32[128,512]{1,0:T(8,128)}, f32[128,512]{1,0:T(8,128)}, f32[2,512]{1,0:T(2,128)}, f32[2,64,512]{2,1,0:T(8,128)}, f32[2,64,512]{2,1,0:T(8,128...) custom-call(f32[128,512]{1,0:T(8,128)} %bitcast.4, ...), custom_call_target="tpu_custom_call" | custom-call | tf_op jit(solution)/shard_map/liquid_layers/pallas_call | solution.py:684
  116.1 5.1 %results.1 = (f32[128,512]{1,0:T(8,128)}, f32[128,512]{1,0:T(8,128)}, f32[2,512]{1,0:T(2,128)}, f32[2,64,512]{2,1,0:T(8,128)}, f32[2,64,512]{2,1,0:T(8,128)}, /*...) custom-call(f32[128,512]{1,0:T(8,128)} %get-tuple-element.36.refs_0_, ...), custom_call_target="tpu_custom_call" | custom-call | tf_op jit(solution)/shard_map/results/pallas_call | solution.py:718

commit v3 on v2

--- a/solution.py
+++ b/solution.py
@@ -17,6 +17,8 @@
 BF16 = jnp.bfloat16
 LANES = 128
 CHUNK = 32
+CHAINS = 6
+UROWS = 256
 EXTRA = 16
 
 
@@ -37,16 +39,24 @@
     return [i for i in range(n.bit_length() - 1)]
 
 
-def orders(seq, batch):
+def orders(seq, batch, chains):
     s = [("seq", b) for b in bits_of(seq)]
     b = [("batch", b) for b in bits_of(batch)]
-    first = s[:1]
-    s, b = s[1:], b
-    one, two = [], []
-    for i in range(max(len(s), len(b))):
-        one += s[i : i + 1] + b[i : i + 1]
-        two += b[i : i + 1] + s[i : i + 1]
-    return [first + one, first + two]
+    near = s[1:2] + b[:2]
+    rest = b[2:] + s[2:]
+    plans = []
+    for c in range(chains):
+        turn = c % len(near)
+        plans.append(s[:1] + near[turn:] + near[:turn] + rest)
+    return plans
+
+
+def chain_rows(rows, devices, most):
+    unit = 8 * devices
+    units = rows // unit
+    chains = min(most, units)
+    cut = [units // chains + (1 if c < units % chains else 0) for c in range(chains)]
+    return [(sum(cut[:c]) * unit, cut[c] * unit) for c in range(chains)]
 
 
 def kernel(cfg, *refs):
@@ -58,8 +68,8 @@
     CB = E2 // LANES
     GROWS = D * CB
     SB_ROWS = 2 * NL + 24
-    plans = orders(S, B)
-    HALF = GROWS // 2
+    spans = chain_rows(GROWS, S * B, CHAINS)
+    plans = orders(S, B, len(spans))
     (
         x_ref, ct_ref, len_ref, gain_ref, dec_hbm, in_hbm, out_hbm, skip_ref, o2_ref, step_ref, w_hbm, bias_ref,
         y_out, gx_out, ggain_out, gdec_out, gin_out, gout_out, gskip_out, go2_out, gstep_out, gw_hbm, gbias_out, stats_out,
@@ -127,8 +137,8 @@
         def __init__(self, l):
             self.l = l
             self.chains = []
-            for c, plan in enumerate(plans):
-                off, size, roff, stages = HALF * c, HALF, 0, []
+            for (base, rows), plan in zip(spans, plans):
+                off, size, roff, stages = base, rows, base, []
                 for i, (axis, bit) in enumerate(plan):
                     half = size // 2
                     mine = my_bit(axis, bit)
@@ -137,21 +147,18 @@
                     stages.append((i, axis, bit, half, keep, give, roff))
                     off, size, roff = keep, half, roff + half
                 self.chains.append(stages)
-            n = len(plans[0])
-            self.n = n
-            self.todo = [functools.partial(self.begin, 0)]
-            for i in range(n):
-                self.todo.append(functools.partial(self.reduce_step, i))
-            for i in range(n - 1, -1, -1):
-                self.todo.append(functools.partial(self.gather_step, i))
+            self.n = n = len(plans[0])
+            self.todo = [self.begin]
+            self.todo += [functools.partial(self.reduce_step, i) for i in range(n)]
+            self.todo += [functools.partial(self.gather_step, i) for i in range(n - 1, -1, -1)]
 
         def rs(self, c, stage):
             i, axis, bit, half, keep, give, roff = stage
             return pltpu.make_async_remote_copy(
                 src_ref=FB.at[self.l, pl.ds(give, half)],
-                dst_ref=RB.at[self.l, c, pl.ds(roff, half)],
-                send_sem=ar_ssem.at[(self.l * 2 + c) * 2, i],
-                recv_sem=ar_rsem.at[(self.l * 2 + c) * 2, i],
+                dst_ref=RB.at[self.l, pl.ds(roff, half)],
+                send_sem=ar_ssem.at[self.l, c, i],
+                recv_sem=ar_rsem.at[self.l, c, i],
                 device_id=swap(axis, bit),
                 device_id_type=MESH,
             )
@@ -161,26 +168,26 @@
             return pltpu.make_async_remote_copy(
                 src_ref=FG.at[self.l, pl.ds(keep, half)],
                 dst_ref=FG.at[self.l, pl.ds(keep, half)],
-                send_sem=ar_ssem.at[(self.l * 2 + c) * 2 + 1, i],
-                recv_sem=ar_rsem.at[(self.l * 2 + c) * 2 + 1, i],
+                send_sem=ar_ssem.at[self.l, c, self.n + i],
+                recv_sem=ar_rsem.at[self.l, c, self.n + i],
                 device_id=swap(axis, bit),
                 device_id_type=MESH,
             )
 
-        def begin(self, i):
+        def begin(self):
             for c, stages in enumerate(self.chains):
-                self.rs(c, stages[i]).start()
+                self.rs(c, stages[0]).start()
 
         def reduce_step(self, i):
             for c, stages in enumerate(self.chains):
                 _, _, _, half, keep, _, roff = stages[i]
                 self.rs(c, stages[i]).wait()
-                step = min(half, 64)
+                step = math.gcd(half, 64)
                 total = FB if i + 1 < self.n else FG
 
                 def add(j, _, keep=keep, roff=roff, step=step, total=total):
                     at = pl.ds(pl.multiple_of(keep + j * step, 8), step)
-                    total[self.l, at, :] = FB[self.l, at, :] + RB[self.l, c, pl.ds(pl.multiple_of(roff + j * step, 8), step), :]
+                    total[self.l, at, :] = FB[self.l, at, :] + RB[self.l, pl.ds(pl.multiple_of(roff + j * step, 8), step), :]
                     return 0
 
                 lax.fori_loop(0, half // step, add, 0)
@@ -195,12 +202,13 @@
                 if i > 0:
                     self.ag(c, stages[i - 1]).start()
                 else:
-                    for q in range(CB // 2):
-                        cb = c * (CB // 2) + q
+                    base, rows = spans[c]
+                    for u in range(base // UROWS, (base + rows) // UROWS):
+                        cb, r = divmod(u * UROWS, D)
                         copy = pltpu.make_async_copy(
-                            FG.at[self.l, pl.ds(cb * D, D)],
-                            gw_hbm.at[self.l, :, pl.ds(cb * LANES, LANES)],
-                            out_sem.at[self.l, cb],
+                            FG.at[self.l, pl.ds(u * UROWS, UROWS)],
+                            gw_hbm.at[self.l, pl.ds(r, UROWS), pl.ds(cb * LANES, LANES)],
+                            out_sem.at[self.l, u],
                         )
                         copy.start()
                         pending.append(copy.wait)
@@ -467,11 +475,12 @@
             def _():
                 seq_copy(l, 3, k, GX.at[tblock(k)], GXR.at[l, me]).start()
 
-            for at, tick in ticks.items():
+            for at, todo in ticks.items():
 
                 @pl.when(kk == at)
-                def _(tick=tick):
-                    tick()
+                def _(todo=todo):
+                    for t in todo:
+                        t.tick()
 
             return nu, acc, gdc, h[0:1, :]
 
@@ -612,33 +621,27 @@
             done()
 
     grads = [gx_out] + [GRD.at[l] for l in range(L - 1)] + [ct_ref]
-    reduces = []
-    smalls = []
+    def at_blocks(plan):
+        return {(q + 1) * S // 4 - 1: todo for q, todo in enumerate(plan) if todo}
+
+    older = []
     for l in range(L - 1, -1, -1):
+        run = lambda things: [t.tick() for t in things]
         glu_backward(l, grads[l + 1])
+        run(older)
         weight_grad(l)
-        mine = Reduce(l)
-        mine.tick()
-        reduces.append(mine)
-
-        def some():
-            for r in reduces + smalls:
-                r.tick()
-
-        ticks = {}
-        if S >= 4:
-            ticks = {S // 4 - 1: some, S // 2 - 1: some, 3 * S // 4 - 1: some}
-        sent = scan_backward(l, ticks)
-        small = Small(l)
+        big, small = Reduce(l), Small(l)
+        big.tick()
+        sent = scan_backward(l, at_blocks([older, [big] + older[1:], older, [big] + older[1:]]))
         small.tick()
-        smalls.append(small)
-        some()
         norm_backward(l, grads[l + 1], grads[l])
         for done in sent:
             done()
-    while any(r.todo for r in reduces + smalls):
-        for r in reduces + smalls:
-            r.tick()
+        run([small, big] + older)
+        older = [big, small] + older
+    while any(t.todo for t in older):
+        for t in older:
+            t.tick()
     for done in pending:
         done()
 
@@ -701,11 +704,11 @@
             buf((L, TA + 1, NL, LANES), F32), buf((TL * 8, LANES), F32), buf((max(TL * 8, TA), LANES), F32),
             buf((L, TL, D), BF16), buf((L, TL, E2), F32), buf((TL, E2), BF16), buf((TL, D), F32),
             buf((L - 1, TL, D), F32), buf((L - 1, TL, D), F32), buf((L, 4, 8, LANES), F32),
-            buf((L, GROWS, LANES), F32), buf((L, 2, GROWS // 2, LANES), F32), buf((L, GROWS, LANES), F32),
+            buf((L, GROWS, LANES), F32), buf((L, GROWS, LANES), F32), buf((L, GROWS, LANES), F32),
             buf((L, NB + 1, SBR, LANES), F32), buf((L, NB, SBR, LANES), F32), buf((L, S, SBR, LANES), F32),
             buf((4, 8, LANES), F32),
-            dma((4,)), dma((L * 4, S)), dma((L * 4, S)), dma((L * 4, NST)), dma((L * 4, NST)),
-            dma((L, NB)), dma((L, NB)), dma((L, S)), dma((L, S)), dma((L, CB)),
+            dma((4,)), dma((L * 4, S)), dma((L * 4, S)), dma((L, CHAINS, 2 * NST)), dma((L, CHAINS, 2 * NST)),
+            dma((L, NB)), dma((L, NB)), dma((L, S)), dma((L, S)), dma((L, GROWS // UROWS)),
         ],
         compiler_params=pltpu.CompilerParams(
             collective_id=0, has_side_effects=True, vmem_limit_bytes=61 * 2**20

time: 121 us -> 114 us (0.942)
  Pallas kernels: 120 us -> 113 us
    pallas_call x1, Pallas kernels: 115 us -> 108 us  [per_device(): pl.pallas_call(functools.partial(kernel, (S, B, TL, D, NS, L, UN)), out_s...]
where the time goes in v3:
time: 114 us
  Pallas kernels  113 us (99%)
  between operations  1.3 us (1%)
    pallas_call x1, Pallas kernels, per_device(): pl.pallas_call(functools.partial(kernel, (S, B, TL, D, NS, L, UN)), out_s...  108 us
    pallas_call x1, Pallas kernels, per_device(): pl.pallas_call(functools.partial(hand_on, len(outs)), out_shape=[shape(o....  5.07 us

profile of v3, /device:TPU:0, one launch (start us, length us, event | category | flops | bytes accessed | tf_op | source)
XLA Modules:
  0.0 114.0 jit_solution(7203021030995122566)
XLA Ops:
  1.3 107.6 %liquid_layers.1 = (f32[128,512]{1,0:T(8,128)}, f32[128,512]{1,0:T(8,128)}, f32[2,512]{1,0:T(2,128)}, f32[2,64,512]{2,1,0:T(8,128)}, f32[2,64,512]{2,1,0:T(8,128...) custom-call(f32[128,512]{1,0:T(8,128)} %bitcast.4, ...), custom_call_target="tpu_custom_call" | custom-call | tf_op jit(solution)/shard_map/liquid_layers/pallas_call | solution.py:687
  108.9 5.1 %results.1 = (f32[128,512]{1,0:T(8,128)}, f32[128,512]{1,0:T(8,128)}, f32[2,512]{1,0:T(2,128)}, f32[2,64,512]{2,1,0:T(8,128)}, f32[2,64,512]{2,1,0:T(8,128)}, /*...) custom-call(f32[128,512]{1,0:T(8,128)} %get-tuple-element.36.refs_0_, ...), custom_call_target="tpu_custom_call" | custom-call | tf_op jit(solution)/shard_map/results/pallas_call | solution.py:721

commit v4 on v3

--- a/solution.py
+++ b/solution.py
@@ -59,6 +59,11 @@
     return [(sum(cut[:c]) * unit, cut[c] * unit) for c in range(chains)]
 
 
+def small_rows(states, batch):
+    unit = 8 * batch
+    return -(-(2 * states + 8 + EXTRA) // unit) * unit
+
+
 def kernel(cfg, *refs):
     S, B, TL, D, NS, L, UN = cfg
     CG = D // LANES
@@ -67,17 +72,17 @@
     E2 = 2 * D
     CB = E2 // LANES
     GROWS = D * CB
-    SB_ROWS = 2 * NL + 24
+    SB_ROWS = small_rows(NL, B)
     spans = chain_rows(GROWS, S * B, CHAINS)
     plans = orders(S, B, len(spans))
     (
         x_ref, ct_ref, len_ref, gain_ref, dec_hbm, in_hbm, out_hbm, skip_ref, o2_ref, step_ref, w_hbm, bias_ref,
-        y_out, gx_out, ggain_out, gdec_out, gin_out, gout_out, gskip_out, go2_out, gstep_out, gw_hbm, gbias_out, stats_out,
+        y_out, gx_out, ggain_out, gdec_out, gin_out, gout_out, gskip_out, go2_out, gstep_out, FG, gbias_out, stats_out,
         W, DEC, INM, OUTM, NA, WT,
         XS, XR, RSTD, R, Y, YR, GS, GMR, GXR,
         SIG, P1, P2, LA, PJ, LG, GA, STR, GRD, ST,
-        FB, RB, FG, SBW, SBR, SBG, VEC,
-        load_sem, send_sem, recv_sem, ar_ssem, ar_rsem, sb_ssem, sb_rsem, sg_ssem, sg_rsem, out_sem,
+        FB, RB, SBW, SBR, SBG, VEC,
+        load_sem, send_sem, recv_sem, ar_ssem, ar_rsem, sb_ssem, sb_rsem, sg_ssem, sg_rsem,
     ) = refs
     U, GX = P2, Y
     me = lax.axis_index("seq")
@@ -201,17 +206,6 @@
                 self.ag(c, stages[i]).wait()
                 if i > 0:
                     self.ag(c, stages[i - 1]).start()
-                else:
-                    base, rows = spans[c]
-                    for u in range(base // UROWS, (base + rows) // UROWS):
-                        cb, r = divmod(u * UROWS, D)
-                        copy = pltpu.make_async_copy(
-                            FG.at[self.l, pl.ds(u * UROWS, UROWS)],
-                            gw_hbm.at[self.l, pl.ds(r, UROWS), pl.ds(cb * LANES, LANES)],
-                            out_sem.at[self.l, u],
-                        )
-                        copy.start()
-                        pending.append(copy.wait)
 
         def tick(self):
             if self.todo:
@@ -344,7 +338,7 @@
         for k, v in enumerate((sq_act, sq_b, sq_s, cnt)):
             ST[l, k] = v
 
-    def glu_backward(l, gsrc):
+    def gate_backward(l, gsrc):
         def gate(i, acc):
             rows = pl.ds(pl.multiple_of(i * CHUNK, CHUNK), CHUNK)
             valid = valid_of(i)
@@ -362,7 +356,9 @@
             return tuple(a + b for a, b in zip(acc, [o[0] for o in out] + [o[1] for o in out]))
 
         zero = jnp.zeros((8, LANES), F32)
-        bias = lax.fori_loop(0, TL // CHUNK, gate, (zero,) * CB)
+        return lax.fori_loop(0, TL // CHUNK, gate, (zero,) * CB)
+
+    def act_backward(l, bias):
         GA[...] = lax.dot_general(LG[...], W[l], (((1,), (1,)), ((), ())), preferred_element_type=F32)
 
         def act(i, _):
@@ -487,39 +483,61 @@
         carry = (zeros, zeros, zeros, jnp.zeros((1, LANES), F32))
         _, acc, gdc, _ = lax.fori_loop(0, S, block, carry)
         sent = [seq_copy(l, 3, me ^ d, GX.at[tblock(me ^ d)], GXR.at[l, me]).wait_send for d in range(1, S)]
-        SBW[l, 0, 0:NL, :] = acc
-        SBW[l, 0, NL : 2 * NL, :] = gdc
+        SBW[l, 0:NL, :] = acc
+        SBW[l, NL : 2 * NL, :] = gdc
         vec = [jnp.sum(VEC[v], axis=0, keepdims=True) for v in range(4)]
         vec += [jnp.zeros((4, LANES), F32)]
-        SBW[l, 0, 2 * NL : 2 * NL + 8, :] = jnp.concatenate(vec, axis=0)
+        SBW[l, 2 * NL : 2 * NL + 8, :] = jnp.concatenate(vec, axis=0)
         extra = GMR[l, 0, TL : TL + EXTRA, :]
         for k in range(1, S):
             extra = extra + GMR[l, k, TL : TL + EXTRA, :]
-        SBW[l, 0, 2 * NL + 8 : 2 * NL + 8 + EXTRA, :] = extra
+        SBW[l, 2 * NL + 8 : 2 * NL + 8 + EXTRA, :] = extra
+        if SB_ROWS > 2 * NL + 8 + EXTRA:
+            SBW[l, 2 * NL + 8 + EXTRA :, :] = jnp.zeros((SB_ROWS - 2 * NL - 8 - EXTRA, LANES), F32)
         return sent
 
     class Small:
         def __init__(self, l):
             self.l = l
-            nb = len(bits_of(B))
-            self.todo = [functools.partial(self.start, 0)]
-            self.todo += [functools.partial(self.join, i) for i in range(nb)]
+            self.n = nb = len(bits_of(B))
+            off, size, roff, self.stages = 0, SB_ROWS, 0, []
+            for i in range(nb):
+                half = size // 2
+                mine = my_bit("batch", i)
+                keep = pl.multiple_of(off + mine * half, 8)
+                give = pl.multiple_of(off + (1 - mine) * half, 8)
+                self.stages.append((i, half, keep, give, roff))
+                off, size, roff = keep, half, roff + half
+            self.todo = [lambda: self.rs(0).start()]
+            self.todo += [functools.partial(self.reduce_step, i) for i in range(nb)]
+            self.todo += [functools.partial(self.gather_step, i) for i in range(nb - 1, -1, -1)]
             self.todo += [self.gathered]
-            self.nb = nb
-
-        def copy(self, i):
+
+        def rs(self, i):
+            _, half, keep, give, roff = self.stages[i]
             return pltpu.make_async_remote_copy(
-                src_ref=SBW.at[self.l, i],
-                dst_ref=SBR.at[self.l, i],
+                src_ref=SBW.at[self.l, pl.ds(give, half)],
+                dst_ref=SBR.at[self.l, pl.ds(roff, half)],
                 send_sem=sb_ssem.at[self.l, i],
                 recv_sem=sb_rsem.at[self.l, i],
                 device_id=(me, bi ^ (1 << i)),
                 device_id_type=MESH,
             )
 
+        def ag(self, i):
+            _, half, keep, give, roff = self.stages[i]
+            return pltpu.make_async_remote_copy(
+                src_ref=SBG.at[self.l, me, pl.ds(keep, half)],
+                dst_ref=SBG.at[self.l, me, pl.ds(keep, half)],
+                send_sem=sb_ssem.at[self.l, self.n + i],
+                recv_sem=sb_rsem.at[self.l, self.n + i],
+                device_id=(me, bi ^ (1 << i)),
+                device_id_type=MESH,
+            )
+
         def seq(self, j, slot, rslot):
             return pltpu.make_async_remote_copy(
-                src_ref=SBW.at[self.l, self.nb],
+                src_ref=SBG.at[self.l, me],
                 dst_ref=SBG.at[self.l, slot],
                 send_sem=sg_ssem.at[self.l, j],
                 recv_sem=sg_rsem.at[self.l, rslot],
@@ -527,18 +545,24 @@
                 device_id_type=MESH,
             )
 
-        def start(self, i):
-            self.copy(i).start()
-
-        def join(self, i):
-            self.copy(i).wait()
-            SBW[self.l, i + 1] = SBW[self.l, i] + SBR[self.l, i]
-            if i + 1 < self.nb:
-                self.start(i + 1)
+        def reduce_step(self, i):
+            _, half, keep, _, roff = self.stages[i]
+            self.rs(i).wait()
+            total = SBW[self.l, pl.ds(keep, half), :] + SBR[self.l, pl.ds(roff, half), :]
+            if i + 1 < self.n:
+                SBW[self.l, pl.ds(keep, half), :] = total
+                self.rs(i + 1).start()
+            else:
+                SBG[self.l, me, pl.ds(keep, half), :] = total
+                self.ag(i).start()
+
+        def gather_step(self, i):
+            self.ag(i).wait()
+            if i > 0:
+                self.ag(i - 1).start()
             else:
                 for d in range(1, S):
                     self.seq(me ^ d, me, me).start()
-                SBG[self.l, me] = SBW[self.l, self.nb]
 
         def gathered(self):
             for d in range(1, S):
@@ -624,44 +648,46 @@
     def at_blocks(plan):
         return {(q + 1) * S // 4 - 1: todo for q, todo in enumerate(plan) if todo}
 
-    older = []
+    run = lambda *things: [t.tick() for t in things]
+    above = ()
     for l in range(L - 1, -1, -1):
-        run = lambda things: [t.tick() for t in things]
-        glu_backward(l, grads[l + 1])
-        run(older)
+        big, small = Reduce(l), Small(l)
+        bias = gate_backward(l, grads[l + 1])
         weight_grad(l)
-        big, small = Reduce(l), Small(l)
-        big.tick()
-        sent = scan_backward(l, at_blocks([older, [big] + older[1:], older, [big] + older[1:]]))
-        small.tick()
+        run(big)
+        run(*above)
+        act_backward(l, bias)
+        plan = [above, (big,), above, (big,)] if above else [(), (big,), (), ()]
+        sent = scan_backward(l, at_blocks(plan))
+        run(small)
         norm_backward(l, grads[l + 1], grads[l])
         for done in sent:
             done()
-        run([small, big] + older)
-        older = [big, small] + older
-    while any(t.todo for t in older):
-        for t in older:
-            t.tick()
+        run(big, *above, small)
+        above = (big, small) + above
+    while any(t.todo for t in above):
+        run(*above)
     for done in pending:
         done()
 
 
-def hand_on(n, *refs):
-    ins, outs, held, sem_in, sem_out = refs[:n], refs[n : 2 * n], refs[2 * n : 3 * n], refs[-2], refs[-1]
-    parts = []
-    for a, o, h in zip(ins, outs, held):
-        if len(a.shape) == 3:
-            parts += [(a.at[l], h.at[l], o.at[l]) for l in range(a.shape[0])]
-        else:
-            parts.append((a, h, o))
-    parts.sort(key=lambda p: math.prod(p[0].shape))
-    for i, (a, h, _) in enumerate(parts):
-        pltpu.make_async_copy(a, h, sem_in.at[i]).start()
-    for i, (a, h, o) in enumerate(parts):
-        pltpu.make_async_copy(a, h, sem_in.at[i]).wait()
-        pltpu.make_async_copy(h, o, sem_out.at[i]).start()
-    for i, (_, h, o) in enumerate(parts):
-        pltpu.make_async_copy(h, o, sem_out.at[i]).wait()
+def hand_on(*refs):
+    n = (len(refs) - 2) // 2
+    sem, block_sem = refs[-2], refs[-1]
+    copies = []
+    for i, (a, o) in enumerate(zip(refs[:n], refs[n : 2 * n])):
+        if a.shape == o.shape:
+            copies.append(pltpu.make_async_copy(a, o, sem.at[i]))
+            continue
+        layers, rows, columns = o.shape
+        for l in range(layers):
+            for c in range(columns // LANES):
+                block = o.at[l, :, pl.ds(c * LANES, LANES)]
+                copies.append(pltpu.make_async_copy(a.at[l, pl.ds(c * rows, rows)], block, block_sem.at[l, c]))
+    for c in copies:
+        c.start()
+    for c in copies:
+        c.wait()
 
 
 def per_device(
@@ -676,7 +702,7 @@
     TA = S * TL
     CB = E2 // LANES
     GROWS = D * CB
-    SBR = 2 * NL + 8 + EXTRA
+    SBR = small_rows(NL, B)
     NB, NST = len(bits_of(B)), len(bits_of(B)) + len(bits_of(S))
     shape = jax.ShapeDtypeStruct
     vmem = pl.BlockSpec(memory_space=pltpu.VMEM)
@@ -687,13 +713,13 @@
     outs = pl.pallas_call(
         functools.partial(kernel, (S, B, TL, D, NS, L, UN)),
         out_shape=[
-            shape((TL, D), F32), shape((TL, D), F32), shape((L, D), F32),
-            shape((L, NS, D), F32), shape((L, NS, D), F32), shape((L, NS, D), F32),
-            shape((L, D), F32), shape((L, D), F32), shape((L, D), F32),
-            shape((L, D, E2), F32), shape((L, E2), F32), shape((L, 3), F32),
+            buf((TL, D), F32), buf((TL, D), F32), buf((L, D), F32),
+            buf((L, NS, D), F32), buf((L, NS, D), F32), buf((L, NS, D), F32),
+            buf((L, D), F32), buf((L, D), F32), buf((L, D), F32),
+            buf((L, GROWS, LANES), F32), buf((L, E2), F32), buf((L, 3), F32),
         ],
         in_specs=[vmem, vmem, smem, vmem, hbm, hbm, hbm, vmem, vmem, vmem, hbm, vmem],
-        out_specs=[vmem] * 9 + [hbm, vmem, vmem],
+        out_specs=[vmem] * 12,
         scratch_shapes=[
             buf((L, D, E2), BF16), buf((L, NS, D), F32), buf((L, NS, D), F32), buf((L, NS, D), F32),
             buf((L, NL, LANES), F32), buf((L, NL, LANES), F32),
@@ -704,14 +730,14 @@
             buf((L, TA + 1, NL, LANES), F32), buf((TL * 8, LANES), F32), buf((max(TL * 8, TA), LANES), F32),
             buf((L, TL, D), BF16), buf((L, TL, E2), F32), buf((TL, E2), BF16), buf((TL, D), F32),
             buf((L - 1, TL, D), F32), buf((L - 1, TL, D), F32), buf((L, 4, 8, LANES), F32),
-            buf((L, GROWS, LANES), F32), buf((L, GROWS, LANES), F32), buf((L, GROWS, LANES), F32),
-            buf((L, NB + 1, SBR, LANES), F32), buf((L, NB, SBR, LANES), F32), buf((L, S, SBR, LANES), F32),
+            buf((L, GROWS, LANES), F32), buf((L, GROWS, LANES), F32),
+            buf((L, SBR, LANES), F32), buf((L, SBR, LANES), F32), buf((L, S, SBR, LANES), F32),
             buf((4, 8, LANES), F32),
             dma((4,)), dma((L * 4, S)), dma((L * 4, S)), dma((L, CHAINS, 2 * NST)), dma((L, CHAINS, 2 * NST)),
-            dma((L, NB)), dma((L, NB)), dma((L, S)), dma((L, S)), dma((L, GROWS // UROWS)),
+            dma((L, 2 * NB)), dma((L, 2 * NB)), dma((L, S)), dma((L, S)),
         ],
         compiler_params=pltpu.CompilerParams(
-            collective_id=0, has_side_effects=True, vmem_limit_bytes=61 * 2**20
+            collective_id=0, has_side_effects=True, vmem_limit_bytes=57 * 2**20
         ),
         name="liquid_layers",
     )(
@@ -719,12 +745,12 @@
         skip_gain, order_two, step_gain, glu_weight, glu_bias,
     )
     outs = pl.pallas_call(
-        functools.partial(hand_on, len(outs)),
-        out_shape=[shape(o.shape, o.dtype) for o in outs],
-        in_specs=[hbm] * len(outs),
+        hand_on,
+        out_shape=[shape((L, D, E2), F32) if o.ndim == 3 and o.shape[1] == GROWS else shape(o.shape, F32) for o in outs],
+        in_specs=[vmem] * len(outs),
         out_specs=[hbm] * len(outs),
-        scratch_shapes=[buf(o.shape, o.dtype) for o in outs] + [dma((2 * len(outs),)), dma((2 * len(outs),))],
-        compiler_params=pltpu.CompilerParams(vmem_limit_bytes=61 * 2**20),
+        scratch_shapes=[dma((len(outs),)), dma((L, CB))],
+        compiler_params=pltpu.CompilerParams(vmem_limit_bytes=2**20),
         name="results",
     )(*outs)
     return (outs[0][None], outs[1][None], *outs[2:])

time: 114 us -> 101 us (0.89)
  Pallas kernels: 113 us -> 99.8 us
    pallas_call x1, Pallas kernels: 108 us -> 97.1 us  [per_device(): pl.pallas_call(functools.partial(kernel, (S, B, TL, D, NS, L, UN)), out_s...]
    pallas_call x1, Pallas kernels: 5.07 us -> 2.67 us  [per_device(): pl.pallas_call(hand_on, out_shape=[shape((L, D, E2), F32) if o.ndim == 3...]
where the time goes in v4:
time: 101 us
  Pallas kernels  99.8 us (99%)
  between operations  1.3 us (1%)
    pallas_call x1, Pallas kernels, per_device(): pl.pallas_call(functools.partial(kernel, (S, B, TL, D, NS, L, UN)), out_s...  97.1 us
    pallas_call x1, Pallas kernels, per_device(): pl.pallas_call(hand_on, out_shape=[shape((L, D, E2), F32) if o.ndim == 3...  2.67 us

profile of v4, /device:TPU:0, one launch (start us, length us, event | category | flops | bytes accessed | tf_op | source)
XLA Modules:
  0.0 101.1 jit_solution(12889392727762297559)
XLA Ops:
  1.3 97.1 %liquid_layers.1 = (f32[128,512]{1,0:T(8,128)S(1)}, f32[128,512]{1,0:T(8,128)S(1)}, f32[2,512]{1,0:T(2,128)S(1)}, f32[2,64,512]{2,1,0:T(8,128)S(1)}, f32[2,64,51...) custom-call(f32[128,512]{1,0:T(8,128)} %bitcast.4, ...), custom_call_target="tpu_custom_call" | custom-call | tf_op jit(solution)/shard_map/liquid_layers/pallas_call | solution.py:713
  98.4 2.7 %results.1 = (f32[128,512]{1,0:T(8,128)}, f32[128,512]{1,0:T(8,128)}, f32[2,512]{1,0:T(2,128)}, f32[2,64,512]{2,1,0:T(8,128)}, f32[2,64,512]{2,1,0:T(8,128)}, /*...) custom-call(f32[128,512]{1,0:T(8,128)S(1)} %get-tuple-element.36.ref, ...), custom_call_target="tpu_custom_call" | custom-call | tf_op jit(solution)/shard_map/results/pallas_call | solution.py:747

commit v5 on v4

v5 whole, which is shorter than its diff:
```python
import functools
import math

import jax
import jax.numpy as jnp
from jax import lax
from jax.experimental import pallas as pl
from jax.experimental.pallas import tpu as pltpu
from jax.sharding import PartitionSpec as P

MESH = pl.DeviceIdType.MESH
EPSILON = 1e-05
LOG2E = 1.4426950408889634
LN2 = 0.6931471805599453
GELU_K = math.sqrt(2.0 / math.pi)
F32 = jnp.float32
BF16 = jnp.bfloat16
LANES = 128
CHUNK = 32
CHAINS = 6
UROWS = 256
PIECES = 4
EXTRA = 16


def rows8(v):
    return v.reshape(v.shape[0] // 8, 8, v.shape[1]).sum(0)


def sigmoid(v):
    return 1.0 / (1.0 + jnp.exp(-v))


def gelu_parts(m):
    th = jnp.tanh(GELU_K * (m + 0.044715 * m * m * m))
    return th


def bits_of(n):
    return [i for i in range(n.bit_length() - 1)]


def orders(seq, batch, chains, spare):
    s = [("seq", b) for b in bits_of(seq)]
    b = [("batch", b) for b in bits_of(batch)]
    near = b[:2] if spare else s[1:2] + b[:2]
    rest = s[1:2] + b[2:] + s[2:] if spare else b[2:] + s[2:]
    plans = []
    for c in range(chains):
        turn = c % len(near)
        plans.append(near[turn:] + near[:turn] + rest)
    return plans


def chain_rows(rows, devices, most):
    unit = 8 * devices
    units = rows // unit
    chains = min(most, units)
    cut = [units // chains + (1 if c < units % chains else 0) for c in range(chains)]
    return [(sum(cut[:c]) * unit, cut[c] * unit) for c in range(chains)]


def small_rows(layers, states, batch):
    unit = 8 * batch
    return -(-layers * (2 * states + EXTRA) // unit) * unit


def kernel(cfg, *refs):
    S, B, TL, D, NS, L, UN = cfg
    CG = D // LANES
    NSP = S // CG
    NL = NS // NSP
    E2 = 2 * D
    CB = E2 // LANES
    GROWS = D * CB
    NQ = PIECES
    TB = TL // NQ
    SB_LAYER = 2 * NL + EXTRA
    SB_ROWS = small_rows(L, NL, B)
    SP = SB_ROWS // B
    spans = chain_rows(GROWS // 2, S * B // 2, CHAINS)
    (
        x_hbm, ct_hbm, len_hbm, gain_hbm, dec_hbm, in_hbm, out_hbm, skip_hbm, o2_hbm, step_hbm, w_hbm, bias_hbm,
        y_out, gx_out, ggain_out, gdec_out, gin_out, gout_out, gskip_out, go2_out, gstep_out, FG, gbias_out, stats_out,
        x_ref, ct_ref, len_ref, gain_ref, DEC, INM, OUTM, skip_ref, o2_ref, step_ref, W, bias_ref, NA, WT,
        XS, XR, RSTD, R, Y, YR, GS, GMR, GXR,
        SIG, P1, P2, LA, PJ, LG, GA, STR, GRD, ST,
        FB, RB, AF, AR, GF, GFR, LA2, LG2, SBW, SBR, SBG, VEC,
        load_sem, send_sem, recv_sem, ar_ssem, ar_rsem, sb_ssem, sb_rsem, sg_ssem, sg_rsem, pair_ssem, pair_rsem,
    ) = refs
    U, GX = P2, Y
    me = lax.axis_index("seq")
    bi = lax.axis_index("batch")
    cg = me // NSP
    nh = lax.rem(me, NSP)
    n0 = nh * NL
    first_part = (nh == 0).astype(F32)
    clane = pl.ds(pl.multiple_of(cg * LANES, LANES), LANES)

    sources = (x_hbm, len_hbm, gain_hbm, o2_hbm, step_hbm, dec_hbm, in_hbm, out_hbm, skip_hbm, w_hbm, bias_hbm, ct_hbm)
    targets = (x_ref, len_ref, gain_ref, o2_ref, step_ref, DEC, INM, OUTM, skip_ref, W, bias_ref, ct_ref)
    loads = [pltpu.make_async_copy(h, v, load_sem.at[i]) for i, (h, v) in enumerate(zip(sources, targets))]
    for c in loads:
        c.start()

    barrier = pltpu.get_barrier_semaphore()
    partners = [(me ^ d, bi) for d in range(1, S)]
    partners += [(me ^ 1, bi ^ (1 << b)) for b in bits_of(B)]
    for p in partners:
        pl.semaphore_signal(barrier, inc=1, device_id=p, device_id_type=MESH)

    sends = []

    def sent():
        while sends:
            sends.pop(0)()

    def seq_copy(ph, j, q, src, dst):
        return pltpu.make_async_remote_copy(
            src_ref=src,
            dst_ref=dst,
            send_sem=send_sem.at[j, q],
            recv_sem=recv_sem.at[ph % 2, me, q],
            device_id=(j, bi),
            device_id_type=MESH,
        )

    def seq_wait(ph, k, q, ref):
        pltpu.make_async_remote_copy(
            src_ref=ref,
            dst_ref=ref,
            send_sem=send_sem.at[k, q],
            recv_sem=recv_sem.at[ph % 2, k, q],
            device_id=(k, bi),
            device_id_type=MESH,
        ).wait_recv()

    def rows_of(q, extra=0):
        return pl.ds(q * TB if isinstance(q, int) else pl.multiple_of(q * TB, TB), TB + extra)

    def span(k, q):
        return pl.ds(pl.multiple_of((k * NQ + q) * TB, TB), TB)

    peers = list(range(S - 1, 0, -1))

    def tblock(k):
        return pl.ds(pl.multiple_of(k * TL, TL), TL)

    def bit_of(v, bit):
        return lax.rem(v // (1 << bit), 2)

    def swap(axis, bit):
        if axis == "batch":
            return (me ^ 1, bi ^ (1 << bit))
        return (me ^ (1 << bit) ^ 1, bi)

    def my_bit(axis, bit):
        return bit_of(me if axis == "seq" else bi, bit)

    side = lax.rem(sum(bit_of(me, i) for i in bits_of(S)) + sum(bit_of(bi, i) for i in bits_of(B)), 2)

    def pair_copy(which, l, src, dst):
        return pltpu.make_async_remote_copy(
            src_ref=src,
            dst_ref=dst,
            send_sem=pair_ssem.at[which],
            recv_sem=pair_rsem.at[which, l],
            device_id=(me ^ 1, bi),
            device_id_type=MESH,
        )

    def act_copy(l):
        return pair_copy(0, l, AF, AR.at[l])

    def grad_copy(l):
        return pair_copy(1, l, GF.at[1 - side], GFR.at[l])

    class Reduce:
        after = ()

        def __init__(self, l):
            self.l = l
            self.chains = []
            plans = orders(S, B, len(spans), False)
            for (base, rows), plan in zip(spans, plans):
                off, size, roff, stages = base, rows, base, []
                for i, (axis, bit) in enumerate(plan):
                    half = size // 2
                    mine = my_bit(axis, bit)
                    keep = pl.multiple_of(off + mine * half, 8)
                    give = pl.multiple_of(off + (1 - mine) * half, 8)
                    stages.append((i, axis, bit, half, keep, give, roff))
                    off, size, roff = keep, half, roff + half
                self.chains.append(stages)
            self.n = n = len(plans[0])
            self.todo = [self.begin]
            self.todo += [functools.partial(self.reduce_step, i) for i in range(n)]
            self.todo += [functools.partial(self.gather_step, i) for i in range(n - 1, -1, -1)]
            self.todo += [self.last_step]

        def rs(self, c, stage):
            i, axis, bit, half, keep, give, roff = stage
            return pltpu.make_async_remote_copy(
                src_ref=FB.at[self.l, pl.ds(give, half)],
                dst_ref=RB.at[self.l, pl.ds(roff, half)],
                send_sem=ar_ssem.at[self.l, c],
                recv_sem=ar_rsem.at[self.l, c, i],
                device_id=swap(axis, bit),
                device_id_type=MESH,
            )

        def pair(self, c):
            base, rows = spans[c]
            here = FG.at[self.l, side, pl.ds(base, rows)]
            return pltpu.make_async_remote_copy(
                src_ref=here,
                dst_ref=here,
                send_sem=ar_ssem.at[self.l, c],
                recv_sem=ar_rsem.at[self.l, c, 2 * self.n],
                device_id=(me ^ 1, bi),
                device_id_type=MESH,
            )

        def ag(self, c, stage):
            i, axis, bit, half, keep, give, roff = stage
            return pltpu.make_async_remote_copy(
                src_ref=FG.at[self.l, side, pl.ds(keep, half)],
                dst_ref=FG.at[self.l, side, pl.ds(keep, half)],
                send_sem=ar_ssem.at[self.l, c],
                recv_sem=ar_rsem.at[self.l, c, self.n + i],
                device_id=swap(axis, bit),
                device_id_type=MESH,
            )

        def begin(self):
            for c, stages in enumerate(self.chains):
                self.rs(c, stages[0]).start()

        def reduce_step(self, i):
            for c, stages in enumerate(self.chains):
                _, _, _, half, keep, _, roff = stages[i]
                self.rs(c, stages[i]).wait()
                step = math.gcd(half, 64)

                def add(j, _, i=i, keep=keep, roff=roff, step=step):
                    at = pl.ds(pl.multiple_of(keep + j * step, 8), step)
                    total = FB[self.l, at, :] + RB[self.l, pl.ds(pl.multiple_of(roff + j * step, 8), step), :]
                    if i + 1 < self.n:
                        FB[self.l, at, :] = total
                    else:
                        FG[self.l, side, at, :] = total
                    return 0

                lax.fori_loop(0, half // step, add, 0)
                if i + 1 < self.n:
                    self.rs(c, stages[i + 1]).start()
                else:
                    self.ag(c, stages[i]).start()

        def gather_step(self, i):
            for c, stages in enumerate(self.chains):
                self.ag(c, stages[i]).wait()
                if i > 0:
                    self.ag(c, stages[i - 1]).start()
                else:
                    self.pair(c).start()

        def last_step(self):
            for c in range(len(self.chains)):
                self.pair(c).wait()

    def norm_forward(l, src):
        def step(i, _):
            rows = pl.ds(pl.multiple_of(i * CHUNK, CHUNK), CHUNK)
            x = src[rows, :]
            center = x - jnp.mean(x, axis=-1, keepdims=True)
            spread = jnp.mean(center * center, axis=-1, keepdims=True)
            inv = lax.rsqrt(spread + EPSILON)
            xhat = center * inv
            RSTD[l, rows, :] = jnp.broadcast_to(inv, (CHUNK, LANES))
            for g in range(CG):
                XS[l, g, rows, :] = xhat[:, g * LANES : (g + 1) * LANES]
            return 0

        lax.fori_loop(0, TL // CHUNK, step, 0)

    def send_normed(l):
        for q in range(NQ):
            for d in peers:
                j = me ^ d
                seq_copy(0, j, q, XS.at[l, j // NSP, rows_of(q)], XR.at[l, span(me, q)]).start()
        XR[l, tblock(me), :] = XS[l, cg]

    def scan_forward(l):
        gain = gain_ref[l : l + 1, clane]
        o2 = o2_ref[l : l + 1, clane]
        stp = step_ref[l : l + 1, clane]
        skip = skip_ref[l : l + 1, clane] * first_part
        first_row = lax.broadcasted_iota(jnp.int32, (TB, LANES), 0) == 0
        SIG[l, 0] = jnp.zeros((NL, LANES), F32)

        def block(b, carry):
            sig, last = carry
            k, q = b // NQ, lax.rem(b, NQ)
            here, t0 = span(k, q), b * TB

            @pl.when(k != me)
            def _():
                seq_wait(0, k, q, XR.at[l, here])

            normed = XR[l, here, :] * gain
            prev = jnp.where(first_row, last, pltpu.roll(normed, 1, 0))
            U[here, :] = normed + o2 * normed * prev
            z = stp * normed
            R[l, here, :] = jnp.maximum(z, 0.0) + jnp.log1p(jnp.exp(-jnp.abs(z)))
            na, wt = NA[l], WT[l]

            def inner(i, sig):
                for s in range(UN):
                    t = i * UN + s
                    at = pl.ds(t0 + t, 1)
                    sig = jnp.exp2(na * R[l, at, :]) * sig + U[at, :]
                    SIG[l, t0 + t + 1] = sig
                    P1[pl.ds(pl.multiple_of(t * 8, 8), 8), :] = rows8(wt * sig)
                return sig

            sig = lax.fori_loop(0, TB // UN, inner, sig)
            for j in range(TB // 8):
                total = P1[pl.ds(j * 64, 8, stride=8), :]
                for s in range(1, 8):
                    total = total + P1[pl.ds(j * 64 + s, 8, stride=8), :]
                at = pl.ds(pl.multiple_of(t0 + j * 8, 8), 8)
                Y[at, :] = total + skip * U[at, :]

            @pl.when(k == me)
            def _():
                YR[l, me, rows_of(q), :] = Y[here, :]

            @pl.when(k != me)
            def _():
                seq_copy(0, k, q, XS.at[l, 0, rows_of(q)], XR.at[l, here]).wait_send()
                seq_copy(1, k, q, Y.at[here], YR.at[l, me, rows_of(q)]).start()

            return sig, normed[TB - 1 : TB, :]

        lax.fori_loop(0, S * NQ, block, (jnp.zeros((NL, LANES), F32), jnp.zeros((1, LANES), F32)))
        for q in range(NQ):
            for d in peers:
                here = span(me ^ d, q)
                sends.append(seq_copy(1, me ^ d, q, Y.at[here], YR.at[l, me, rows_of(q)]).wait_send)

    def mixed_of(l, g, rows):
        m = YR[l, g * NSP, rows, :]
        for h in range(1, NSP):
            m = m + YR[l, g * NSP + h, rows, :]
        return m

    def valid_of(i):
        pos = me * TL + i * CHUNK + lax.broadcasted_iota(jnp.int32, (CHUNK, 1), 0)
        return (pos < len_ref[0]).astype(F32)

    def glu_forward(l, src, dst):
        for q in range(NQ):
            for d in peers:
                seq_wait(1, me ^ d, q, YR.at[l, me ^ d, rows_of(q)])

        def act(i, sq):
            rows = pl.ds(pl.multiple_of(i * CHUNK, CHUNK), CHUNK)
            valid = valid_of(i)
            for g in range(CG):
                m = mixed_of(l, g, rows)
                a = 0.5 * m * (1.0 + gelu_parts(m))
                low = a.astype(BF16)
                LA[l, rows, g * LANES : (g + 1) * LANES] = low
                AF[rows, g * LANES : (g + 1) * LANES] = low.astype(F32)
                sq = sq + rows8(a * a * valid)
            return sq

        zero = jnp.zeros((8, LANES), F32)
        if l:
            act_copy(l - 1).wait_send()
        sq_act = lax.fori_loop(0, TL // CHUNK, act, zero)
        act_copy(l).start()
        PJ[l] = jnp.dot(LA[l], W[l], preferred_element_type=F32) + bias_ref[l : l + 1, :]

        def gate(i, sq):
            sq_b, sq_s, cnt = sq
            rows = pl.ds(pl.multiple_of(i * CHUNK, CHUNK), CHUNK)
            valid = valid_of(i)
            for g in range(CG):
                cols = slice(g * LANES, (g + 1) * LANES)
                gcols = slice(D + g * LANES, D + (g + 1) * LANES)
                branch = PJ[l, rows, cols] * sigmoid(PJ[l, rows, gcols]) * valid
                out = src[rows, cols] + branch
                dst[rows, cols] = out
                sq_b = sq_b + rows8(branch * branch)
                sq_s = sq_s + rows8(out * out * valid)
            cnt = cnt + rows8(jnp.broadcast_to(valid, (CHUNK, LANES)))
            return sq_b, sq_s, cnt

        sq_b, sq_s, cnt = lax.fori_loop(0, TL // CHUNK, gate, (zero, zero, zero))
        for k, v in enumerate((sq_act, sq_b, sq_s, cnt)):
            ST[l, k] = v

    def gate_backward(l, gsrc):
        def gate(i, acc):
            rows = pl.ds(pl.multiple_of(i * CHUNK, CHUNK), CHUNK)
            valid = valid_of(i)
            out = []
            for g in range(CG):
                cols = slice(g * LANES, (g + 1) * LANES)
                gcols = slice(D + g * LANES, D + (g + 1) * LANES)
                gb = gsrc[rows, cols] * valid
                s = sigmoid(PJ[l, rows, gcols])
                one = gb * s
                two = one * PJ[l, rows, cols] * (1.0 - s)
                low_one, low_two = one.astype(BF16), two.astype(BF16)
                LG[rows, cols] = low_one
                LG[rows, gcols] = low_two
                GF[0, rows, cols] = low_one.astype(F32)
                GF[1, rows, cols] = low_two.astype(F32)
                out.append((rows8(one), rows8(two)))
            return tuple(a + b for a, b in zip(acc, [o[0] for o in out] + [o[1] for o in out]))

        zero = jnp.zeros((8, LANES), F32)
        if l < L - 1:
            grad_copy(l + 1).wait_send()
        bias = lax.fori_loop(0, TL // CHUNK, gate, (zero,) * CB)
        grad_copy(l).start()
        return bias

    def act_backward(l, bias):
        GA[...] = lax.dot_general(LG[...], W[l], (((1,), (1,)), ((), ())), preferred_element_type=F32)

        def act(i, _):
            rows = pl.ds(pl.multiple_of(i * CHUNK, CHUNK), CHUNK)
            for g in range(CG):
                m = mixed_of(l, g, rows)
                th = gelu_parts(m)
                slope = 0.5 * (1.0 + th) + 0.5 * m * (1.0 - th * th) * GELU_K * (1.0 + 3 * 0.044715 * m * m)
                GS[l, g, rows, :] = GA[rows, g * LANES : (g + 1) * LANES] * slope
            return 0

        lax.fori_loop(0, TL // CHUNK, act, 0)
        extra = [jnp.sum(b, axis=0, keepdims=True) for b in bias]
        extra += [jnp.sum(ST[l, k], axis=0, keepdims=True) for k in range(4)]
        extra += [jnp.zeros((EXTRA - len(extra), LANES), F32)]
        extra = jnp.concatenate(extra, axis=0)
        for g in range(CG):
            GS[l, g, TL : TL + EXTRA, :] = extra
        for q in range(NQ - 1, -1, -1):
            rows = rows_of(q, EXTRA if q == NQ - 1 else 0)
            for d in peers:
                j = me ^ d
                seq_copy(2, j, q, GS.at[l, j // NSP, rows], GMR.at[l, me, rows]).start()
        GMR[l, me] = GS[l, cg]

    def weight_grad(l):
        if l == L - 1:
            act_copy(l).wait_send()
        act_copy(l).wait_recv()
        grad_copy(l).wait_recv()

        def cast(i, _):
            rows = pl.ds(pl.multiple_of(i * CHUNK, CHUNK), CHUNK)
            also = pl.ds(pl.multiple_of(TL + i * CHUNK, CHUNK), CHUNK)
            LA2[rows, :] = LA[l, rows, :]
            LA2[also, :] = AR[l, rows, :].astype(BF16)
            LG2[rows, :] = GF[side, rows, :].astype(BF16)
            LG2[also, :] = GFR[l, rows, :].astype(BF16)
            return 0

        lax.fori_loop(0, TL // CHUNK, cast, 0)
        half = lax.dot_general(LA2[...], LG2[...], (((0,), (0,)), ((), ())), preferred_element_type=F32)
        for q in range(CB // 2):
            FB[l, pl.ds(q * D, D), :] = half[:, q * LANES : (q + 1) * LANES]

    def scan_backward(l, steps):
        gain = gain_ref[l : l + 1, clane]
        o2 = o2_ref[l : l + 1, clane]
        stp = step_ref[l : l + 1, clane]
        skip = skip_ref[l : l + 1, clane]
        row_id = lax.broadcasted_iota(jnp.int32, (TB, LANES), 0)
        zero8 = jnp.zeros((8, LANES), F32)
        zeros = jnp.zeros((NL, LANES), F32)
        for v in range(4):
            VEC[v] = zero8

        def with_grads(k, q, what):
            for last in (False, True):

                @pl.when((k != me) & ((q == NQ - 1) == last))
                def _():
                    what(rows_of(NQ - 1, EXTRA) if last else rows_of(q))

        def block(bb, carry):
            nu, acc, gdc, after = carry
            b = S * NQ - 1 - bb
            k, q = b // NQ, lax.rem(b, NQ)
            here, t0 = span(k, q), b * TB
            with_grads(k, q, lambda rows: seq_wait(2, k, q, GMR.at[l, k, rows]))
            na, wt = NA[l], WT[l]

            def inner(ii, c):
                nu, acc, gdc = c
                i = TB // UN - 1 - ii
                for s in range(UN - 1, -1, -1):
                    t = i * UN + s
                    logs = na * R[l, pl.ds(t0 + t, 1), :]
                    gm = GMR[l, k, pl.ds(q * TB + t, 1), :]
                    mu = wt * gm + nu
                    if l == 0:
                        acc = acc + gm * SIG[l, t0 + t + 1]
                    at = pl.ds(pl.multiple_of(t * 8, 8), 8)
                    P1[at, :] = rows8(mu)
                    nu = jnp.exp2(logs) * mu
                    part = nu * SIG[l, t0 + t] * logs
                    gdc = gdc + part
                    P2[at, :] = rows8(part)
                return nu, acc, gdc

            nu, acc, gdc = lax.fori_loop(0, TB // UN, inner, (nu, acc, gdc))
            for j in range(TB // 8):
                one = P1[pl.ds(j * 64, 8, stride=8), :]
                two = P2[pl.ds(j * 64, 8, stride=8), :]
                for s in range(1, 8):
                    one = one + P1[pl.ds(j * 64 + s, 8, stride=8), :]
                    two = two + P2[pl.ds(j * 64 + s, 8, stride=8), :]
                GX[pl.ds(pl.multiple_of(t0 + j * 8, 8), 8), :] = one
                GA[j * 8 : j * 8 + 8, 0:LANES] = two
            xhat = XR[l, here, :]
            normed = xhat * gain
            before = XR[l, pl.ds(jnp.maximum(t0 - 1, 0), 1), :] * gain
            before = jnp.where(b == 0, 0.0, before)
            prev = jnp.where(row_id == 0, before, pltpu.roll(normed, 1, 0))
            gm = GMR[l, k, rows_of(q), :] * first_part
            gdrv = GX[here, :] + skip * gm
            both = gdrv * normed
            h = o2 * both
            later = jnp.where(row_id == TB - 1, after, pltpu.roll(h, TB - 1, 0))
            rate = R[l, here, :]
            some = rate > 1e-30
            ratio = jnp.where(some, sigmoid(stp * normed) / jnp.where(some, rate, 1.0), 1.0)
            slope = GA[0:TB, 0:LANES] * LN2 * ratio
            gnormed = gdrv * (1.0 + o2 * prev) + later + slope * stp
            GX[here, :] = gnormed * gain
            VEC[0] = VEC[0] + rows8(gm * (normed + o2 * normed * prev))
            VEC[1] = VEC[1] + rows8(both * prev)
            VEC[2] = VEC[2] + rows8(slope * normed)
            VEC[3] = VEC[3] + rows8(gnormed * xhat)

            @pl.when(k == me)
            def _():
                GXR[l, me, rows_of(q), :] = GX[here, :]

            with_grads(k, q, lambda rows: seq_copy(2, k, q, GS.at[l, 0, rows], GMR.at[l, me, rows]).wait_send())

            @pl.when(k != me)
            def _():
                seq_copy(3, k, q, GX.at[here], GXR.at[l, me, rows_of(q)]).start()

            for place in sorted(steps):

                @pl.when(bb == place)
                def _(todo=steps[place]):
                    for step in todo:
                        step()

            return nu, acc, gdc, h[0:1, :]

        carry = (zeros, zeros, zeros, jnp.zeros((1, LANES), F32))
        _, acc, gdc, _ = lax.fori_loop(0, S * NQ, block, carry)
        for q in range(NQ):
            for d in peers:
                here = span(me ^ d, q)
                sends.append(seq_copy(3, me ^ d, q, GX.at[here], GXR.at[l, me, rows_of(q)]).wait_send)
        gdc = gdc / NA[l]
        base = l * SB_LAYER
        SBW[base + NL : base + 2 * NL, :] = gdc
        if l == 0:
            SBW[base : base + NL, :] = acc
        vec = [jnp.sum(VEC[v], axis=0, keepdims=True) for v in range(4)]
        SBW[base + 2 * NL : base + 2 * NL + 4, :] = jnp.concatenate(vec, axis=0)
        extra = GMR[l, 0, TL : TL + 12, :]
        for k in range(1, S):
            extra = extra + GMR[l, k, TL : TL + 12, :]
        SBW[base + 2 * NL + 4 : base + SB_LAYER, :] = extra

    def late_sum(l):
        def step(i, acc):
            for s in range(8):
                t = i * 8 + s
                acc = acc + GMR[l, i // (TL // 8), pl.ds(lax.rem(i, TL // 8) * 8 + s, 1), :] * SIG[l, t + 1]
            return acc

        SBW[l * SB_LAYER : l * SB_LAYER + NL, :] = lax.fori_loop(0, S * TL // 8, step, jnp.zeros((NL, LANES), F32))

    class Small:
        def __init__(self, first):
            self.after = [(first, first.n)]
            self.todo = [self.begin, self.join, self.across]
            self.todo += [functools.partial(self.along, i) for i in range(len(bits_of(S)))]

        def part(self, j):
            return pl.ds(pl.multiple_of(j * SP, 8), SP)

        def rs(self, j, slot):
            return pltpu.make_async_remote_copy(
                src_ref=SBW.at[self.part(j)],
                dst_ref=SBR.at[slot],
                send_sem=sb_ssem.at[j],
                recv_sem=sb_rsem.at[0, slot],
                device_id=(me, j),
                device_id_type=MESH,
            )

        def ag(self, j, slot):
            rows = self.part(slot)
            return pltpu.make_async_remote_copy(
                src_ref=SBG.at[me, rows],
                dst_ref=SBG.at[me, rows],
                send_sem=sb_ssem.at[j],
                recv_sem=sb_rsem.at[1, slot],
                device_id=(me, j),
                device_id_type=MESH,
            )

        def seq(self, i, slot):
            return pltpu.make_async_remote_copy(
                src_ref=SBG.at[slot],
                dst_ref=SBG.at[slot],
                send_sem=sg_ssem.at[slot],
                recv_sem=sg_rsem.at[slot],
                device_id=(me ^ (S >> (i + 1)), bi),
                device_id_type=MESH,
            )

        def begin(self):
            if SB_ROWS > L * SB_LAYER:
                SBW[L * SB_LAYER :, :] = jnp.zeros((SB_ROWS - L * SB_LAYER, LANES), F32)
            for d in range(B - 1, 0, -1):
                self.rs(bi ^ d, bi).start()
            SBR[bi] = SBW[self.part(bi), :]

        def join(self):
            for d in range(B - 1, 0, -1):
                self.rs(bi ^ d, bi ^ d).wait()
            total = SBR[0]
            for j in range(1, B):
                total = total + SBR[j]
            SBG[me, self.part(bi), :] = total
            for d in range(B - 1, 0, -1):
                self.ag(bi ^ d, bi).start()

        def across(self):
            for d in range(B - 1, 0, -1):
                self.ag(bi ^ d, bi ^ d).wait()
            self.seq(0, me).start()

        def slots(self, i):
            held = [me]
            for k in range(i):
                held = held + [slot ^ (S >> (k + 1)) for slot in held]
            return held

        def along(self, i):
            step = S >> (i + 1)
            for slot in self.slots(i):
                self.seq(i, slot).wait_send()
                self.seq(i, slot ^ step).wait_recv()
            if i + 1 < len(bits_of(S)):
                for slot in self.slots(i + 1):
                    self.seq(i + 1, slot).start()
            else:
                for l in range(L):
                    self.gathered(l)

        def gathered(self, l):
            base = l * SB_LAYER
            for g in range(CG):
                cols = slice(g * LANES, (g + 1) * LANES)
                vec = None
                for h in range(NSP):
                    slot = g * NSP + h
                    rows = slice(h * NL, (h + 1) * NL)
                    acc = SBG[slot, base : base + NL, :]
                    gin_out[l, rows, cols] = OUTM[l, rows, cols] * acc
                    gout_out[l, rows, cols] = INM[l, rows, cols] * acc
                    gdec_out[l, rows, cols] = -SBG[slot, base + NL : base + 2 * NL, :]
                    part = SBG[slot, base + 2 * NL : base + 2 * NL + 4, :]
                    vec = part if vec is None else vec + part
                gskip_out[l : l + 1, cols] = vec[0:1]
                go2_out[l : l + 1, cols] = vec[1:2]
                gstep_out[l : l + 1, cols] = vec[2:3]
                ggain_out[l : l + 1, cols] = vec[3:4]
            base += 2 * NL + 4
            for q in range(CB):
                gbias_out[l : l + 1, q * LANES : (q + 1) * LANES] = SBG[0, base + q : base + q + 1, :]
            sq = jnp.sum(SBG[0, base + CB : base + CB + 4, :], axis=1, keepdims=True)
            count = sq[3:4] * (1.0 / LANES)
            root = jnp.sqrt(sq[0:3] / (count * D))
            col = lax.broadcasted_iota(jnp.int32, (1, 3), 1)
            stats_out[l : l + 1, :] = jnp.where(col == 0, root[0:1], jnp.where(col == 1, root[1:2], root[2:3]))

    def norm_backward(l, gsrc, gdst):
        for q in range(NQ):
            for d in peers:
                seq_wait(3, me ^ d, q, GXR.at[l, me ^ d, rows_of(q)])

        def step(i, _):
            rows = pl.ds(pl.multiple_of(i * CHUNK, CHUNK), CHUNK)
            inv = RSTD[l, rows, :]
            gx, xh = [], []
            s1 = s2 = None
            for g in range(CG):
                v = GXR[l, g * NSP, rows, :]
                for h in range(1, NSP):
                    v = v + GXR[l, g * NSP + h, rows, :]
                x = XS[l, g, rows, :]
                gx.append(v)
                xh.append(x)
                s1 = v if s1 is None else s1 + v
                s2 = v * x if s2 is None else s2 + v * x
            m1 = jnp.sum(s1, axis=-1, keepdims=True) * (1.0 / D)
            m2 = jnp.sum(s2, axis=-1, keepdims=True) * (1.0 / D)
            for g in range(CG):
                cols = slice(g * LANES, (g + 1) * LANES)
                gdst[rows, cols] = gsrc[rows, cols] + inv * (gx[g] - m1 - xh[g] * m2)
            return 0

        lax.fori_loop(0, TL // CHUNK, step, 0)

    loads[0].wait()
    norm_forward(0, x_ref)
    pl.semaphore_wait(barrier, len(partners))
    send_normed(0)
    for c in loads[1:]:
        c.wait()
    nrows = pl.ds(pl.multiple_of(n0, 8), NL)
    for l in range(L):
        NA[l] = DEC[l, nrows, clane] * (-LOG2E)
        WT[l] = INM[l, nrows, clane] * OUTM[l, nrows, clane]
    streams = [x_ref] + [STR.at[l] for l in range(L - 1)] + [y_out]
    for l in range(L):
        if l:
            norm_forward(l, streams[l])
            send_normed(l)
        scan_forward(l)
        glu_forward(l, streams[l], streams[l + 1])
        sent()

    grads = [gx_out] + [GRD.at[l] for l in range(L - 1)] + [ct_ref]
    def take(things):
        steps = []
        for t in things:
            if t.todo and all(len(a.todo) <= left for a, left in t.after):
                steps.append(t.todo.pop(0))
        return steps

    def run(*things):
        for step in take(things):
            step()

    def places(plan):
        return {(i + 1) * S * NQ // len(plan) - 1: take(things) for i, things in enumerate(plan) if things}

    bigs = []
    for l in range(L - 1, -1, -1):
        bias = gate_backward(l, grads[l + 1])
        act_backward(l, bias)
        weight_grad(l)
        above = list(bigs)
        bigs.insert(0, Reduce(l))
        run(bigs[0])
        if above:
            late_sum(l + 1)
            scan_backward(l, places([above, bigs[:1], above, bigs[:1], above, [], [], bigs[:1]]))
        else:
            scan_backward(l, places([[], bigs, [], []]))
        if l == 0:
            small = Small(bigs[-1])
            run(small)
        norm_backward(l, grads[l + 1], grads[l])
        sent()
        run(*bigs)
    grad_copy(0).wait_send()
    while any(t.todo for t in bigs + [small]):
        run(bigs[0], small, *bigs[1:])


def hand_on(*refs):
    n = (len(refs) - 2) // 2
    sem, block_sem = refs[-2], refs[-1]
    copies = []
    for i, (a, o) in enumerate(zip(refs[:n], refs[n : 2 * n])):
        if a.shape == o.shape:
            copies.append(pltpu.make_async_copy(a, o, sem.at[i]))
            continue
        layers, rows, columns = o.shape
        for l in range(layers):
            for c in range(columns // LANES):
                block = o.at[l, :, pl.ds(c * LANES, LANES)]
                side, at = divmod(c * rows, a.shape[2])
                copies.append(pltpu.make_async_copy(a.at[l, side, pl.ds(at, rows)], block, block_sem.at[l, c]))
    for c in copies:
        c.start()
    for c in copies:
        c.wait()


def per_device(
    stream_in, cotangent, lengths, norm_gain, decay_rate, in_map, out_map, skip_gain, order_two, step_gain, glu_weight, glu_bias
):
    S, B = lax.axis_size("seq"), lax.axis_size("batch")
    _, TL, D = stream_in.shape
    L, NS = decay_rate.shape[:2]
    UN = math.gcd(TL // PIECES, 32)
    CG, E2 = D // LANES, 2 * D
    NL = NS // (S // CG)
    TA = S * TL
    CB = E2 // LANES
    GROWS = D * CB
    SBR = small_rows(L, NL, B)
    NB, NST = len(bits_of(B)), len(bits_of(B)) + len(bits_of(S))
    shape = jax.ShapeDtypeStruct
    vmem = pl.BlockSpec(memory_space=pltpu.VMEM)
    hbm = pl.BlockSpec(memory_space=pl.ANY)
    buf = pltpu.VMEM
    dma = pltpu.SemaphoreType.DMA
    outs = pl.pallas_call(
        functools.partial(kernel, (S, B, TL, D, NS, L, UN)),
        out_shape=[
            buf((TL, D), F32), buf((TL, D), F32), buf((L, D), F32),
            buf((L, NS, D), F32), buf((L, NS, D), F32), buf((L, NS, D), F32),
            buf((L, D), F32), buf((L, D), F32), buf((L, D), F32),
            buf((L, 2, GROWS // 2, LANES), F32), buf((L, E2), F32), buf((L, 3), F32),
        ],
        in_specs=[hbm] * 12,
        out_specs=[vmem] * 12,
        scratch_shapes=[
            buf((TL, D), F32), buf((TL, D), F32), pltpu.SMEM((1,), jnp.int32), buf((L, D), F32),
            buf((L, NS, D), F32), buf((L, NS, D), F32), buf((L, NS, D), F32),
            buf((L, D), F32), buf((L, D), F32), buf((L, D), F32), buf((L, D, E2), BF16), buf((L, E2), F32),
            buf((L, NL, LANES), F32), buf((L, NL, LANES), F32),
            buf((L, CG, TL, LANES), F32), buf((L, TA, LANES), F32), buf((L, TL, LANES), F32),
            buf((L, TA, LANES), F32), buf((TA, LANES), F32),
            buf((L, S, TL, LANES), F32), buf((L, CG, TL + EXTRA, LANES), F32), buf((L, S, TL + EXTRA, LANES), F32),
            buf((L, S, TL, LANES), F32),
            buf((L, TA + 1, NL, LANES), F32), buf((TL * 8, LANES), F32), buf((max(TL * 8, TA), LANES), F32),
            buf((L, TL, D), BF16), buf((L, TL, E2), F32), buf((TL, E2), BF16), buf((TL, D), F32),
            buf((L - 1, TL, D), F32), buf((L - 1, TL, D), F32), buf((L, 4, 8, LANES), F32),
            buf((L, GROWS // 2, LANES), F32), buf((L, GROWS // 2, LANES), F32),
            buf((TL, D), F32), buf((L, TL, D), F32), buf((2, TL, D), F32), buf((L, TL, D), F32), buf((2 * TL, D), BF16), buf((2 * TL, D), BF16),
            buf((SBR, LANES), F32), buf((B, SBR // B, LANES), F32), buf((S, SBR, LANES), F32),
            buf((4, 8, LANES), F32),
            dma((12,)), dma((S, PIECES)), dma((2, S, PIECES)), dma((L, CHAINS)), dma((L, CHAINS, 2 * NST - 1)),
            dma((B,)), dma((2, B)), dma((S,)), dma((S,)), dma((2,)), dma((2, L)),
        ],
        compiler_params=pltpu.CompilerParams(
            collective_id=0, has_side_effects=True, vmem_limit_bytes=57 * 2**20
        ),
        name="liquid_layers",
    )(
        stream_in[0], cotangent[0], lengths, norm_gain, decay_rate, in_map, out_map,
        skip_gain, order_two, step_gain, glu_weight, glu_bias,
    )
    outs = pl.pallas_call(
        hand_on,
        out_shape=[shape((L, D, E2), F32) if o.ndim == 4 else shape(o.shape, F32) for o in outs],
        in_specs=[vmem] * len(outs),
        out_specs=[hbm] * len(outs),
        scratch_shapes=[dma((len(outs),)), dma((L, CB))],
        compiler_params=pltpu.CompilerParams(vmem_limit_bytes=2**20),
        name="results",
    )(*outs)
    return (outs[0][None], outs[1][None], *outs[2:])


def solution(mesh):
    split = P("batch", "seq", None)
    in_specs = (split, split, P("batch")) + (P(),) * 9
    out_specs = (split, split) + (P(),) * 10
    return jax.shard_map(per_device, mesh=mesh, in_specs=in_specs, out_specs=out_specs, check_vma=False)
```

time: 101 us -> 93.2 us (0.923)
  Pallas kernels: 99.8 us -> 91.7 us
    pallas_call x1, Pallas kernels: 97.1 us -> 89.1 us  [per_device(): pl.pallas_call(functools.partial(kernel, (S, B, TL, D, NS, L, UN)), out_s...]
where the time goes in v5:
time: 93.2 us; the launch traced here: 93 us
  Pallas kernels  91.7 us (98%)
  between operations  1.3 us (1%)
    pallas_call x1, Pallas kernels, per_device(): pl.pallas_call(functools.partial(kernel, (S, B, TL, D, NS, L, UN)), out_s...  89.1 us
    pallas_call x1, Pallas kernels, per_device(): pl.pallas_call(hand_on, out_shape=[shape((L, D, E2), F32) if o.ndim == 4...  2.67 us

profile of v5, /device:TPU:0, one launch (start us, length us, event | category | flops | bytes accessed | tf_op | source)
XLA Modules:
  0.0 93.0 jit_solution(10859986597111203367)
XLA Ops:
  1.3 89.1 %liquid_layers.1 = (f32[128,512]{1,0:T(8,128)S(1)}, f32[128,512]{1,0:T(8,128)S(1)}, f32[2,512]{1,0:T(2,128)S(1)}, f32[2,64,512]{2,1,0:T(8,128)S(1)}, f32[2,64,51...) custom-call(f32[128,512]{1,0:T(8,128)} %bitcast.4, ...), custom_call_target="tpu_custom_call" | custom-call | tf_op jit(solution)/shard_map/liquid_layers/pallas_call | solution.py:830
  90.4 2.7 %results.1 = (f32[128,512]{1,0:T(8,128)}, f32[128,512]{1,0:T(8,128)}, f32[2,512]{1,0:T(2,128)}, f32[2,64,512]{2,1,0:T(8,128)}, f32[2,64,512]{2,1,0:T(8,128)}, /*...) custom-call(f32[128,512]{1,0:T(8,128)S(1)} %get-tuple-element.36.ref, ...), custom_call_target="tpu_custom_call" | custom-call | tf_op jit(solution)/shard_map/results/pallas_call | solution.py:867

commit v6 on v5

--- a/solution.py
+++ b/solution.py
@@ -40,16 +40,12 @@
     return [i for i in range(n.bit_length() - 1)]
 
 
-def orders(seq, batch, chains, spare):
+def orders(seq, batch, chains, upper):
     s = [("seq", b) for b in bits_of(seq)]
     b = [("batch", b) for b in bits_of(batch)]
-    near = b[:2] if spare else s[1:2] + b[:2]
-    rest = s[1:2] + b[2:] + s[2:] if spare else b[2:] + s[2:]
-    plans = []
-    for c in range(chains):
-        turn = c % len(near)
-        plans.append(near[turn:] + near[:turn] + rest)
-    return plans
+    x, y, z, rest = s[1:2], b[:1], b[1:2], b[2:] + s[2:]
+    kinds = [y + z + x, z + y + x] if upper else [x + y + z, y + z + x, z + x + y]
+    return [kinds[c % len(kinds)] + rest for c in range(chains)]
 
 
 def chain_rows(rows, devices, most):
@@ -135,8 +131,8 @@
             device_id_type=MESH,
         ).wait_recv()
 
-    def rows_of(q, extra=0):
-        return pl.ds(q * TB if isinstance(q, int) else pl.multiple_of(q * TB, TB), TB + extra)
+    def rows_of(q):
+        return pl.ds(q * TB if isinstance(q, int) else pl.multiple_of(q * TB, TB), TB)
 
     def span(k, q):
         return pl.ds(pl.multiple_of((k * NQ + q) * TB, TB), TB)
@@ -181,7 +177,7 @@
         def __init__(self, l):
             self.l = l
             self.chains = []
-            plans = orders(S, B, len(spans), False)
+            plans = orders(S, B, len(spans), l > 0)
             for (base, rows), plan in zip(spans, plans):
                 off, size, roff, stages = base, rows, base, []
                 for i, (axis, bit) in enumerate(plan):
@@ -223,9 +219,10 @@
 
         def ag(self, c, stage):
             i, axis, bit, half, keep, give, roff = stage
+            here = FG.at[self.l, side, pl.ds(keep, half)]
             return pltpu.make_async_remote_copy(
-                src_ref=FG.at[self.l, side, pl.ds(keep, half)],
-                dst_ref=FG.at[self.l, side, pl.ds(keep, half)],
+                src_ref=here,
+                dst_ref=here,
                 send_sem=ar_ssem.at[self.l, c],
                 recv_sem=ar_rsem.at[self.l, c, self.n + i],
                 device_id=swap(axis, bit),
@@ -332,10 +329,6 @@
                 at = pl.ds(pl.multiple_of(t0 + j * 8, 8), 8)
                 Y[at, :] = total + skip * U[at, :]
 
-            @pl.when(k == me)
-            def _():
-                YR[l, me, rows_of(q), :] = Y[here, :]
-
             @pl.when(k != me)
             def _():
                 seq_copy(0, k, q, XS.at[l, 0, rows_of(q)], XR.at[l, here]).wait_send()
@@ -344,6 +337,7 @@
             return sig, normed[TB - 1 : TB, :]
 
         lax.fori_loop(0, S * NQ, block, (jnp.zeros((NL, LANES), F32), jnp.zeros((1, LANES), F32)))
+        YR[l, me] = Y[tblock(me), :]
         for q in range(NQ):
             for d in peers:
                 here = span(me ^ d, q)
@@ -442,18 +436,15 @@
             return 0
 
         lax.fori_loop(0, TL // CHUNK, act, 0)
-        extra = [jnp.sum(b, axis=0, keepdims=True) for b in bias]
-        extra += [jnp.sum(ST[l, k], axis=0, keepdims=True) for k in range(4)]
-        extra += [jnp.zeros((EXTRA - len(extra), LANES), F32)]
-        extra = jnp.concatenate(extra, axis=0)
-        for g in range(CG):
-            GS[l, g, TL : TL + EXTRA, :] = extra
         for q in range(NQ - 1, -1, -1):
-            rows = rows_of(q, EXTRA if q == NQ - 1 else 0)
             for d in peers:
                 j = me ^ d
-                seq_copy(2, j, q, GS.at[l, j // NSP, rows], GMR.at[l, me, rows]).start()
+                seq_copy(2, j, q, GS.at[l, j // NSP, rows_of(q)], GMR.at[l, me, rows_of(q)]).start()
         GMR[l, me] = GS[l, cg]
+        extra = list(bias) + [ST[l, k] for k in range(4)]
+        extra = jnp.concatenate([jnp.sum(v, axis=0, keepdims=True) for v in extra], axis=0)
+        base = l * SB_LAYER + 2 * NL + 4
+        SBW[base : base + len(bias) + 4, :] = extra
 
     def weight_grad(l):
         if l == L - 1:
@@ -486,19 +477,16 @@
         for v in range(4):
             VEC[v] = zero8
 
-        def with_grads(k, q, what):
-            for last in (False, True):
-
-                @pl.when((k != me) & ((q == NQ - 1) == last))
-                def _():
-                    what(rows_of(NQ - 1, EXTRA) if last else rows_of(q))
-
         def block(bb, carry):
             nu, acc, gdc, after = carry
             b = S * NQ - 1 - bb
             k, q = b // NQ, lax.rem(b, NQ)
             here, t0 = span(k, q), b * TB
-            with_grads(k, q, lambda rows: seq_wait(2, k, q, GMR.at[l, k, rows]))
+
+            @pl.when(k != me)
+            def _():
+                seq_wait(2, k, q, GMR.at[l, k, rows_of(q)])
+
             na, wt = NA[l], WT[l]
 
             def inner(ii, c):
@@ -549,27 +537,28 @@
             VEC[2] = VEC[2] + rows8(slope * normed)
             VEC[3] = VEC[3] + rows8(gnormed * xhat)
 
-            @pl.when(k == me)
-            def _():
-                GXR[l, me, rows_of(q), :] = GX[here, :]
-
-            with_grads(k, q, lambda rows: seq_copy(2, k, q, GS.at[l, 0, rows], GMR.at[l, me, rows]).wait_send())
-
             @pl.when(k != me)
             def _():
+                seq_copy(2, k, q, GS.at[l, 0, rows_of(q)], GMR.at[l, me, rows_of(q)]).wait_send()
                 seq_copy(3, k, q, GX.at[here], GXR.at[l, me, rows_of(q)]).start()
 
-            for place in sorted(steps):
-
-                @pl.when(bb == place)
-                def _(todo=steps[place]):
-                    for step in todo:
-                        step()
+            if steps:
+                hit = functools.reduce(jnp.logical_or, [bb == place for place in sorted(steps)])
+
+                @pl.when(hit)
+                def _():
+                    for place in sorted(steps):
+
+                        @pl.when(bb == place)
+                        def _(todo=steps[place]):
+                            for step in todo:
+                                step()
 
             return nu, acc, gdc, h[0:1, :]
 
         carry = (zeros, zeros, zeros, jnp.zeros((1, LANES), F32))
         _, acc, gdc, _ = lax.fori_loop(0, S * NQ, block, carry)
+        GXR[l, me] = GX[tblock(me), :]
         for q in range(NQ):
             for d in peers:
                 here = span(me ^ d, q)
@@ -581,10 +570,6 @@
             SBW[base : base + NL, :] = acc
         vec = [jnp.sum(VEC[v], axis=0, keepdims=True) for v in range(4)]
         SBW[base + 2 * NL : base + 2 * NL + 4, :] = jnp.concatenate(vec, axis=0)
-        extra = GMR[l, 0, TL : TL + 12, :]
-        for k in range(1, S):
-            extra = extra + GMR[l, k, TL : TL + 12, :]
-        SBW[base + 2 * NL + 4 : base + SB_LAYER, :] = extra
 
     def late_sum(l):
         def step(i, acc):
@@ -597,7 +582,7 @@
 
     class Small:
         def __init__(self, first):
-            self.after = [(first, first.n)]
+            self.after = [(first, first.n + 1)]
             self.todo = [self.begin, self.join, self.across]
             self.todo += [functools.partial(self.along, i) for i in range(len(bits_of(S)))]
 
@@ -694,9 +679,12 @@
                 gstep_out[l : l + 1, cols] = vec[2:3]
                 ggain_out[l : l + 1, cols] = vec[3:4]
             base += 2 * NL + 4
+            extra = SBG[0, base : base + CB + 4, :]
+            for k in range(1, S):
+                extra = extra + SBG[k, base : base + CB + 4, :]
             for q in range(CB):
-                gbias_out[l : l + 1, q * LANES : (q + 1) * LANES] = SBG[0, base + q : base + q + 1, :]
-            sq = jnp.sum(SBG[0, base + CB : base + CB + 4, :], axis=1, keepdims=True)
+                gbias_out[l : l + 1, q * LANES : (q + 1) * LANES] = extra[q : q + 1]
+            sq = jnp.sum(extra[CB:], axis=1, keepdims=True)
             count = sq[3:4] * (1.0 / LANES)
             root = jnp.sqrt(sq[0:3] / (count * D))
             col = lax.broadcasted_iota(jnp.int32, (1, 3), 1)
@@ -762,7 +750,7 @@
             step()
 
     def places(plan):
-        return {(i + 1) * S * NQ // len(plan) - 1: take(things) for i, things in enumerate(plan) if things}
+        return {(i + 1) * S * NQ // 16 - 1: take(plan[i]) for i in sorted(plan)}
 
     bigs = []
     for l in range(L - 1, -1, -1):
@@ -774,9 +762,9 @@
         run(bigs[0])
         if above:
             late_sum(l + 1)
-            scan_backward(l, places([above, bigs[:1], above, bigs[:1], above, [], [], bigs[:1]]))
+            scan_backward(l, places({5: above, 12: above, 13: bigs[:1]}))
         else:
-            scan_backward(l, places([[], bigs, [], []]))
+            scan_backward(l, places({11: bigs}))
         if l == 0:
             small = Small(bigs[-1])
             run(small)
@@ -844,7 +832,7 @@
             buf((L, NL, LANES), F32), buf((L, NL, LANES), F32),
             buf((L, CG, TL, LANES), F32), buf((L, TA, LANES), F32), buf((L, TL, LANES), F32),
             buf((L, TA, LANES), F32), buf((TA, LANES), F32),
-            buf((L, S, TL, LANES), F32), buf((L, CG, TL + EXTRA, LANES), F32), buf((L, S, TL + EXTRA, LANES), F32),
+            buf((L, S, TL, LANES), F32), buf((L, CG, TL, LANES), F32), buf((L, S, TL, LANES), F32),
             buf((L, S, TL, LANES), F32),
             buf((L, TA + 1, NL, LANES), F32), buf((TL * 8, LANES), F32), buf((max(TL * 8, TA), LANES), F32),
             buf((L, TL, D), BF16), buf((L, TL, E2), F32), buf((TL, E2), BF16), buf((TL, D), F32),

time: 93.2 us -> 91.1 us (0.977)
  Pallas kernels: 91.7 us -> 89.6 us
    pallas_call x1, Pallas kernels: 89.1 us -> 87 us  [per_device(): pl.pallas_call(functools.partial(kernel, (S, B, TL, D, NS, L, UN)), out_s...]
where the time goes in v6:
time: 91.1 us; the launch traced here: 90.9 us
  Pallas kernels  89.6 us (98%)
  between operations  1.3 us (1%)
    pallas_call x1, Pallas kernels, per_device(): pl.pallas_call(functools.partial(kernel, (S, B, TL, D, NS, L, UN)), out_s...  87 us
    pallas_call x1, Pallas kernels, per_device(): pl.pallas_call(hand_on, out_shape=[shape((L, D, E2), F32) if o.ndim == 4...  2.67 us

profile of v6, /device:TPU:0, one launch (start us, length us, event | category | flops | bytes accessed | tf_op | source)
XLA Modules:
  0.0 90.9 jit_solution(11348377487929012030)
XLA Ops:
  1.3 87.0 %liquid_layers.1 = (f32[128,512]{1,0:T(8,128)S(1)}, f32[128,512]{1,0:T(8,128)S(1)}, f32[2,512]{1,0:T(2,128)S(1)}, f32[2,64,512]{2,1,0:T(8,128)S(1)}, f32[2,64,51...) custom-call(f32[128,512]{1,0:T(8,128)} %bitcast.4, ...), custom_call_target="tpu_custom_call" | custom-call | tf_op jit(solution)/shard_map/liquid_layers/pallas_call | solution.py:818
  88.3 2.7 %results.1 = (f32[128,512]{1,0:T(8,128)}, f32[128,512]{1,0:T(8,128)}, f32[2,512]{1,0:T(2,128)}, f32[2,64,512]{2,1,0:T(8,128)}, f32[2,64,512]{2,1,0:T(8,128)}, /*...) custom-call(f32[128,512]{1,0:T(8,128)S(1)} %get-tuple-element.36.ref, ...), custom_call_target="tpu_custom_call" | custom-call | tf_op jit(solution)/shard_map/results/pallas_call | solution.py:855

commit v7 on v6

--- a/solution.py
+++ b/solution.py
@@ -44,7 +44,7 @@
     s = [("seq", b) for b in bits_of(seq)]
     b = [("batch", b) for b in bits_of(batch)]
     x, y, z, rest = s[1:2], b[:1], b[1:2], b[2:] + s[2:]
-    kinds = [y + z + x, z + y + x] if upper else [x + y + z, y + z + x, z + x + y]
+    kinds = [y + z + x, z + y + x] if upper else [y + z + x, z + x + y, x + y + z]
     return [kinds[c % len(kinds)] + rest for c in range(chains)]
 
 
@@ -212,7 +212,7 @@
                 src_ref=here,
                 dst_ref=here,
                 send_sem=ar_ssem.at[self.l, c],
-                recv_sem=ar_rsem.at[self.l, c, 2 * self.n],
+                recv_sem=ar_rsem.at[self.l, c, self.n + 1],
                 device_id=(me ^ 1, bi),
                 device_id_type=MESH,
             )
@@ -224,7 +224,7 @@
                 src_ref=here,
                 dst_ref=here,
                 send_sem=ar_ssem.at[self.l, c],
-                recv_sem=ar_rsem.at[self.l, c, self.n + i],
+                recv_sem=ar_rsem.at[self.l, c, i - 1 if i else self.n],
                 device_id=swap(axis, bit),
                 device_id_type=MESH,
             )
@@ -841,7 +841,7 @@
             buf((TL, D), F32), buf((L, TL, D), F32), buf((2, TL, D), F32), buf((L, TL, D), F32), buf((2 * TL, D), BF16), buf((2 * TL, D), BF16),
             buf((SBR, LANES), F32), buf((B, SBR // B, LANES), F32), buf((S, SBR, LANES), F32),
             buf((4, 8, LANES), F32),
-            dma((12,)), dma((S, PIECES)), dma((2, S, PIECES)), dma((L, CHAINS)), dma((L, CHAINS, 2 * NST - 1)),
+            dma((12,)), dma((S, PIECES)), dma((2, S, PIECES)), dma((L, CHAINS)), dma((L, CHAINS, NST + 1)),
             dma((B,)), dma((2, B)), dma((S,)), dma((S,)), dma((2,)), dma((2, L)),
         ],
         compiler_params=pltpu.CompilerParams(

time: 91.1 us -> 90.1 us (0.989)
  Pallas kernels: 89.6 us -> 88.6 us
    pallas_call x1, Pallas kernels: 87 us -> 86 us  [per_device(): pl.pallas_call(functools.partial(kernel, (S, B, TL, D, NS, L, UN)), out_s...]
where the time goes in v7:
time: 90.1 us; the launch traced here: 89.9 us
  Pallas kernels  88.6 us (98%)
  between operations  1.3 us (1%)
    pallas_call x1, Pallas kernels, per_device(): pl.pallas_call(functools.partial(kernel, (S, B, TL, D, NS, L, UN)), out_s...  86 us
    pallas_call x1, Pallas kernels, per_device(): pl.pallas_call(hand_on, out_shape=[shape((L, D, E2), F32) if o.ndim == 4...  2.67 us

profile of v7, /device:TPU:0, one launch (start us, length us, event | category | flops | bytes accessed | tf_op | source)
XLA Modules:
  0.0 89.9 jit_solution(14605440800651893120)
XLA Ops:
  1.3 86.0 %liquid_layers.1 = (f32[128,512]{1,0:T(8,128)S(1)}, f32[128,512]{1,0:T(8,128)S(1)}, f32[2,512]{1,0:T(2,128)S(1)}, f32[2,64,512]{2,1,0:T(8,128)S(1)}, f32[2,64,51...) custom-call(f32[128,512]{1,0:T(8,128)} %bitcast.4, ...), custom_call_target="tpu_custom_call" | custom-call | tf_op jit(solution)/shard_map/liquid_layers/pallas_call | solution.py:818
  87.3 2.7 %results.1 = (f32[128,512]{1,0:T(8,128)}, f32[128,512]{1,0:T(8,128)}, f32[2,512]{1,0:T(2,128)}, f32[2,64,512]{2,1,0:T(8,128)}, f32[2,64,512]{2,1,0:T(8,128)}, /*...) custom-call(f32[128,512]{1,0:T(8,128)S(1)} %get-tuple-element.36.ref, ...), custom_call_target="tpu_custom_call" | custom-call | tf_op jit(solution)/shard_map/results/pallas_call | solution.py:855

commit v8 on v7

--- a/solution.py
+++ b/solution.py
@@ -266,9 +266,9 @@
             for c in range(len(self.chains)):
                 self.pair(c).wait()
 
-    def norm_forward(l, src):
-        def step(i, _):
-            rows = pl.ds(pl.multiple_of(i * CHUNK, CHUNK), CHUNK)
+    def norm_forward(l, src, done=lambda q: None):
+        def step(i):
+            rows = pl.ds(i * CHUNK, CHUNK)
             x = src[rows, :]
             center = x - jnp.mean(x, axis=-1, keepdims=True)
             spread = jnp.mean(center * center, axis=-1, keepdims=True)
@@ -277,16 +277,17 @@
             RSTD[l, rows, :] = jnp.broadcast_to(inv, (CHUNK, LANES))
             for g in range(CG):
                 XS[l, g, rows, :] = xhat[:, g * LANES : (g + 1) * LANES]
-            return 0
-
-        lax.fori_loop(0, TL // CHUNK, step, 0)
-
-    def send_normed(l):
+
         for q in range(NQ):
-            for d in peers:
-                j = me ^ d
-                seq_copy(0, j, q, XS.at[l, j // NSP, rows_of(q)], XR.at[l, span(me, q)]).start()
-        XR[l, tblock(me), :] = XS[l, cg]
+            for i in range(q * TB // CHUNK, (q + 1) * TB // CHUNK):
+                step(i)
+            done(q)
+
+    def send_normed(l, q):
+        for d in peers:
+            j = me ^ d
+            seq_copy(0, j, q, XS.at[l, j // NSP, rows_of(q)], XR.at[l, span(me, q)]).start()
+        XR[l, span(me, q), :] = XS[l, cg, rows_of(q), :]
 
     def scan_forward(l):
         gain = gain_ref[l : l + 1, clane]
@@ -426,17 +427,17 @@
     def act_backward(l, bias):
         GA[...] = lax.dot_general(LG[...], W[l], (((1,), (1,)), ((), ())), preferred_element_type=F32)
 
-        def act(i, _):
-            rows = pl.ds(pl.multiple_of(i * CHUNK, CHUNK), CHUNK)
+        def act(i):
+            rows = pl.ds(i * CHUNK, CHUNK)
             for g in range(CG):
                 m = mixed_of(l, g, rows)
                 th = gelu_parts(m)
                 slope = 0.5 * (1.0 + th) + 0.5 * m * (1.0 - th * th) * GELU_K * (1.0 + 3 * 0.044715 * m * m)
                 GS[l, g, rows, :] = GA[rows, g * LANES : (g + 1) * LANES] * slope
-            return 0
-
-        lax.fori_loop(0, TL // CHUNK, act, 0)
+
         for q in range(NQ - 1, -1, -1):
+            for i in range(q * TB // CHUNK, (q + 1) * TB // CHUNK):
+                act(i)
             for d in peers:
                 j = me ^ d
                 seq_copy(2, j, q, GS.at[l, j // NSP, rows_of(q)], GMR.at[l, me, rows_of(q)]).start()
@@ -721,7 +722,8 @@
     loads[0].wait()
     norm_forward(0, x_ref)
     pl.semaphore_wait(barrier, len(partners))
-    send_normed(0)
+    for q in range(NQ):
+        send_normed(0, q)
     for c in loads[1:]:
         c.wait()
     nrows = pl.ds(pl.multiple_of(n0, 8), NL)
@@ -731,8 +733,7 @@
     streams = [x_ref] + [STR.at[l] for l in range(L - 1)] + [y_out]
     for l in range(L):
         if l:
-            norm_forward(l, streams[l])
-            send_normed(l)
+            norm_forward(l, streams[l], functools.partial(send_normed, l))
         scan_forward(l)
         glu_forward(l, streams[l], streams[l + 1])
         sent()

time: 90.1 us -> 89.6 us (level)
  no operation moved by 1% of the time
where the time goes in v8:
time: 89.6 us; the launch traced here: 89.5 us
  Pallas kernels  88.2 us (98%)
  between operations  1.3 us (1%)
    pallas_call x1, Pallas kernels, per_device(): pl.pallas_call(functools.partial(kernel, (S, B, TL, D, NS, L, UN)), out_s...  85.5 us
    pallas_call x1, Pallas kernels, per_device(): pl.pallas_call(hand_on, out_shape=[shape((L, D, E2), F32) if o.ndim == 4...  2.67 us

profile of v8, /device:TPU:0, one launch (start us, length us, event | category | flops | bytes accessed | tf_op | source)
XLA Modules:
  0.0 89.5 jit_solution(15816221557214349106)
XLA Ops:
  1.3 85.5 %liquid_layers.1 = (f32[128,512]{1,0:T(8,128)S(1)}, f32[128,512]{1,0:T(8,128)S(1)}, f32[2,512]{1,0:T(2,128)S(1)}, f32[2,64,512]{2,1,0:T(8,128)S(1)}, f32[2,64,51...) custom-call(f32[128,512]{1,0:T(8,128)} %bitcast.4, ...), custom_call_target="tpu_custom_call" | custom-call | tf_op jit(solution)/shard_map/liquid_layers/pallas_call | solution.py:819
  86.8 2.7 %results.1 = (f32[128,512]{1,0:T(8,128)}, f32[128,512]{1,0:T(8,128)}, f32[2,512]{1,0:T(2,128)}, f32[2,64,512]{2,1,0:T(8,128)}, f32[2,64,512]{2,1,0:T(8,128)}, /*...) custom-call(f32[128,512]{1,0:T(8,128)S(1)} %get-tuple-element.36.ref, ...), custom_call_target="tpu_custom_call" | custom-call | tf_op jit(solution)/shard_map/results/pallas_call | solution.py:856
